TPU v7x, 32 devices: a whole 2x2x4 slice. The times are simulated.
32 devices in a mesh: dp: 8 (over z, y), mp: 4 (over x, core).
Axes of the slice: x: 2, y: 2, z: 4, core: 2. Of those that a mesh axis runs over, the one named last changes fastest.
Arguments:
- latents: float32 [16, 20, 1024], P('dp', None, 'mp'), may hold values from -6 to 6
- noise_draw: float32 [16, 20, 1024], P('dp', None, 'mp'), may hold values from -6 to 6
- timesteps: int32 [16], P('dp'), may hold values from 60 to 519
- text_ids: int32 [16, 128], P('dp'), may hold values from 0 to 32127
- text_len: int32 [16], P('dp'), may hold values from 1 to 128, as said below
- item_counts: int32 [8], P('dp'), may hold values from 1 to 2, as said below
- text_table: bfloat16 [32128, 768], P('mp'), may hold values from -6 to 6
- io_weight: float32 [2, 20, 1024], P(None, None, 'dp'), may hold values from -4 to 4
- io_first: float32 [2, 20, 1024], P(None, None, 'dp'), may hold values from -2.9802322e-07 to 2.9802322e-07
- io_second: float32 [2, 20, 1024], P(None, None, 'dp'), may hold values from 3.0718206e-17 to 1.2287282e-16
- io_average: float32 [2, 20, 1024], P(None, None, 'dp'), may hold values from -4 to 4
- norm_gains: float32 [7, 1024], P(None, 'dp'), may hold values from 0.2 to 3
- gains_first: float32 [7, 1024], P(None, 'dp'), may hold values from -1.1920929e-06 to 1.1920929e-06
- gains_second: float32 [7, 1024], P(None, 'dp'), may hold values from 4.914913e-16 to 1.9659652e-15
- gains_average: float32 [7, 1024], P(None, 'dp'), may hold values from 0.2 to 3
- col_weight: float32 [2, 1024, 8, 1024], P(None, 'dp', None, 'mp'), may hold values from -0.1875 to 0.1875
- col_first: float32 [2, 1024, 8, 1024], P(None, 'dp', None, 'mp'), may hold values from -2.9802322e-07 to 2.9802322e-07
- col_second: float32 [2, 1024, 8, 1024], P(None, 'dp', None, 'mp'), may hold values from 3.0718206e-17 to 1.2287282e-16
- col_average: float32 [2, 1024, 8, 1024], P(None, 'dp', None, 'mp'), may hold values from -0.1875 to 0.1875
- text_weight: float32 [2, 768, 2, 1024], P(None, 'dp', None, 'mp'), may hold values from -0.21875 to 0.21875
- text_first: float32 [2, 768, 2, 1024], P(None, 'dp', None, 'mp'), may hold values from -2.9802322e-07 to 2.9802322e-07
- text_second: float32 [2, 768, 2, 1024], P(None, 'dp', None, 'mp'), may hold values from 3.0718206e-17 to 1.2287282e-16
- text_average: float32 [2, 768, 2, 1024], P(None, 'dp', None, 'mp'), may hold values from -0.21875 to 0.21875
- row_weight: float32 [2, 6, 1024, 1024], P(None, None, 'dp', 'mp'), may hold values from -3 to 3
- row_first: float32 [2, 6, 1024, 1024], P(None, None, 'dp', 'mp'), may hold values from -2.9802322e-07 to 2.9802322e-07
- row_second: float32 [2, 6, 1024, 1024], P(None, None, 'dp', 'mp'), may hold values from 3.8397757e-18 to 1.5359103e-17
- row_average: float32 [2, 6, 1024, 1024], P(None, None, 'dp', 'mp'), may hold values from -3 to 3
Outputs:
- loss_sum: float32 [], replicated
- item_total: float32 [], replicated
- grad_norm: float32 [], replicated
- io_weight_new: float32 [2, 20, 1024], P(None, None, 'dp')
- io_first_new: float32 [2, 20, 1024], P(None, None, 'dp')
- in_second_new: float32 [20, 1024], P(None, 'dp')
- out_second_new: float32 [20, 1024], P(None, 'dp')
- io_average_new: float32 [2, 20, 1024], P(None, None, 'dp')
- norm_gains_new: float32 [7, 1024], P(None, 'dp')
- gains_first_new: float32 [7, 1024], P(None, 'dp')
- gains_second_new: float32 [7, 1024], P(None, 'dp')
- gains_average_new: float32 [7, 1024], P(None, 'dp')
- col_weight_new: float32 [2, 1024, 8, 1024], P(None, 'dp', None, 'mp')
- col_first_new: float32 [2, 1024, 8, 1024], P(None, 'dp', None, 'mp')
- col_second_new: float32 [2, 1024, 8, 1024], P(None, 'dp', None, 'mp')
- col_average_new: float32 [2, 1024, 8, 1024], P(None, 'dp', None, 'mp')
- text_weight_new: float32 [2, 768, 2, 1024], P(None, 'dp', None, 'mp')
- text_first_new: float32 [2, 768, 2, 1024], P(None, 'dp', None, 'mp')
- text_second_new: float32 [2, 768, 2, 1024], P(None, 'dp', None, 'mp')
- text_average_new: float32 [2, 768, 2, 1024], P(None, 'dp', None, 'mp')
- row_weight_new: float32 [2, 6, 1024, 1024], P(None, None, 'dp', 'mp')
- row_first_new: float32 [2, 6, 1024, 1024], P(None, None, 'dp', 'mp')
- row_second_new: float32 [2, 6, 1024, 1024], P(None, None, 'dp', 'mp')
- row_average_new: float32 [2, 6, 1024, 1024], P(None, None, 'dp', 'mp')
Inputs may be any that keep to these rules, and one draw needn't show every extreme that they name: `text_len`: some item of the batch has all 128 caption tokens. `item_counts`: some index of dp holds 2 real items; real items take the lowest slots.
All inputs are finite; a program needn't handle non-finite values.
Results may differ from a plain program's by a relative error of at most 0.018.
Values may be sent and summed in bfloat16 or wider, within the bound.
A program may use at most 384 MiB of HBM per device.

v0:
```python
import math

import jax
import jax.numpy as jnp
from jax import lax
from jax.sharding import PartitionSpec as P

HEAD_DIM = 64
STEP = 10


norm_eps = 1e-06
clip_limit = 0.001
matrix_rate = 0.04
gain_rate = 0.6
row_rate = 0.1
beta_first = 0.9
beta_second = 0.999
adam_eps = 1e-08
weight_decay = 0.01
average_keep = 0.5
snr_limit = 5.0


def as_low(tensor):
    return tensor.astype(jnp.bfloat16)


def sinusoid(position, width):
    half_width = width // 2
    frequency = jnp.exp(-math.log(10000.0) * jnp.arange(half_width, dtype=jnp.float32) / half_width)
    angles = position[..., None] * frequency
    return jnp.concatenate([jnp.sin(angles), jnp.cos(angles)], axis=-1)


def plan():
    beta_table = jnp.linspace(0.00085**0.5, 0.012**0.5, 1000, dtype=jnp.float32) ** 2
    return jnp.cumprod(1.0 - beta_table)


def gelu_tanh(inputs):
    return jax.nn.gelu(inputs, approximate=True)


def layer_norm(inputs, gain):
    centre = inputs - jnp.mean(inputs, -1, keepdims=True)
    inverse = lax.rsqrt(jnp.mean(centre * centre, -1, keepdims=True) + norm_eps)
    normed = centre * inverse
    return (normed * gain, normed, inverse)


def norm_back(upstream, gain, normed, inverse):
    scaled = upstream * gain
    inputs_grad = inverse * (
        scaled
        - jnp.mean(scaled, -1, keepdims=True)
        - normed * jnp.mean(scaled * normed, -1, keepdims=True)
    )
    return (inputs_grad, jnp.sum(upstream * normed, axis=(0, 1)))


def gather_rows(tensor):
    return lax.all_gather(tensor, "mp", axis=1, tiled=True)


def sum_rows(tensor):
    return lax.psum_scatter(
        tensor.astype(jnp.bfloat16), "mp", scatter_dimension=1, tiled=True
    ).astype(jnp.float32)


def gather_grads(tensor):
    return lax.all_gather(as_low(tensor), "mp", axis=1, tiled=True)


def sum_grads(tensor):
    return lax.psum_scatter(
        tensor.astype(jnp.bfloat16), "mp", scatter_dimension=1, tiled=True
    ).astype(jnp.float32)


def query_blocks(tensor, blocks):
    items, frames = (tensor.shape[0], tensor.shape[1])
    return jnp.swapaxes(tensor.reshape((items, blocks, frames // blocks) + tensor.shape[2:]), 0, 1)


def block_scores(query_part, keys_in, allowed, score_scale):
    scores = (
        jnp.einsum("iqhe,ikhe->ihqk", query_part, keys_in, preferred_element_type=jnp.float32)
        * score_scale
    )
    return jnp.where(allowed[:, None, None, :], scores, -1e30)


def attend_forward(queries, keys_in, values_in, allowed, score_scale):
    frames = queries.shape[1]
    blocks = frames // min(512, frames)

    def one_block(query_part):
        scores = block_scores(query_part, keys_in, allowed, score_scale)
        largest = jnp.max(scores, -1, keepdims=True)
        exp_scores = jnp.exp(scores - largest)
        totals = jnp.sum(exp_scores, -1, keepdims=True)
        result = jnp.einsum(
            "ihqk,ikhe->iqhe",
            as_low(exp_scores / totals),
            values_in,
            preferred_element_type=jnp.float32,
        )
        return (as_low(result), (largest + jnp.log(totals))[..., 0])

    outputs, log_totals = lax.map(one_block, query_blocks(queries, blocks))
    return (jnp.swapaxes(outputs, 0, 1).reshape(queries.shape), log_totals)


def attend_backward(queries, keys_in, values_in, allowed, score_scale, log_totals, out_grad):
    frames = queries.shape[1]
    blocks = frames // min(512, frames)

    def one_block(carry, pieces):
        query_part, grad_part, log_part = pieces
        scores = block_scores(query_part, keys_in, allowed, score_scale)
        probs_full = jnp.exp(scores - log_part[..., None])
        prob_grad = jnp.einsum(
            "iqhe,ikhe->ihqk", grad_part, values_in, preferred_element_type=jnp.float32
        )
        score_grad = as_low(
            probs_full * (prob_grad - jnp.sum(probs_full * prob_grad, -1, keepdims=True))
        )
        query_grad = (
            jnp.einsum("ihqk,ikhe->iqhe", score_grad, keys_in, preferred_element_type=jnp.float32)
            * score_scale
        )
        key_grad = (
            carry[0]
            + jnp.einsum(
                "ihqk,iqhe->ikhe", score_grad, query_part, preferred_element_type=jnp.float32
            )
            * score_scale
        )
        value_grad = carry[1] + jnp.einsum(
            "ihqk,iqhe->ikhe", as_low(probs_full), grad_part, preferred_element_type=jnp.float32
        )
        return ((key_grad, value_grad), query_grad)

    zero_carry = (jnp.zeros(keys_in.shape, jnp.float32), jnp.zeros(values_in.shape, jnp.float32))
    (key_grad, value_grad), query_grad = lax.scan(
        one_block,
        zero_carry,
        (query_blocks(queries, blocks), query_blocks(out_grad, blocks), log_totals),
    )
    return (jnp.swapaxes(query_grad, 0, 1).reshape(queries.shape), key_grad, value_grad)


def layer_forward(resid, weights, layer_index, text_feat, allowed):
    gain_w = weights[1].astype(jnp.float32)
    col_w = weights[2][layer_index]
    kv_w = weights[3][layer_index]
    row_w = weights[4][layer_index]
    items = resid.shape[0]
    head_count = col_w.shape[-1] // HEAD_DIM
    score_scale = HEAD_DIM ** (-0.5)
    normed_out, normed_self, inverse_self = layer_norm(resid, gain_w[3 * layer_index])
    whole_self = gather_rows(as_low(normed_out))
    frames = whole_self.shape[1]
    projected = as_low(
        jnp.einsum("ifd,dsc->ifsc", whole_self, col_w[:, 0:3], preferred_element_type=jnp.float32)
    )
    split_heads = projected.reshape(items, frames, 3, head_count, HEAD_DIM)
    self_query = split_heads[:, :, 0]
    self_keys = split_heads[:, :, 1]
    self_values = split_heads[:, :, 2]
    all_keys = jnp.ones((items, self_keys.shape[1]), bool)
    attended, self_log = attend_forward(self_query, self_keys, self_values, all_keys, score_scale)
    attended = attended.reshape(items, frames, -1)
    resid = resid + sum_rows(
        jnp.einsum("ifc,dc->ifd", attended, row_w[0], preferred_element_type=jnp.float32)
    )
    normed_out, normed_cross, inverse_cross = layer_norm(resid, gain_w[3 * layer_index + 1])
    whole_cross = gather_rows(as_low(normed_out))
    cross_query = as_low(
        jnp.einsum("ifd,dc->ifc", whole_cross, col_w[:, 3], preferred_element_type=jnp.float32)
    )
    text_proj = as_low(
        jnp.einsum("itd,dsc->itsc", text_feat, kv_w, preferred_element_type=jnp.float32)
    )
    text_heads = text_proj.reshape(items, text_feat.shape[1], 2, head_count, HEAD_DIM)
    cross_out, cross_log = attend_forward(
        cross_query.reshape(items, frames, head_count, HEAD_DIM),
        text_heads[:, :, 0],
        text_heads[:, :, 1],
        allowed,
        score_scale,
    )
    cross_out = cross_out.reshape(items, frames, -1)
    resid = resid + sum_rows(
        jnp.einsum("ifc,dc->ifd", cross_out, row_w[1], preferred_element_type=jnp.float32)
    )
    normed_out, normed_mlp, inverse_mlp = layer_norm(resid, gain_w[3 * layer_index + 2])
    whole_mlp = gather_rows(as_low(normed_out))
    hidden = jnp.einsum(
        "ifd,dsc->ifsc", whole_mlp, col_w[:, 4:8], preferred_element_type=jnp.float32
    )
    active = as_low(gelu_tanh(hidden))
    resid = resid + sum_rows(
        jnp.einsum("ifsc,sdc->ifd", active, row_w[2:6], preferred_element_type=jnp.float32)
    )
    kept_values = (
        normed_self,
        inverse_self,
        whole_self,
        (self_query, self_keys, self_values),
        attended,
        self_log,
        normed_cross,
        inverse_cross,
        whole_cross,
        cross_query,
        text_heads,
        cross_out,
        cross_log,
        normed_mlp,
        inverse_mlp,
        whole_mlp,
        hidden,
        active,
    )
    return (resid, kept_values)


def layer_backward(resid_grad, weights, layer_index, text_feat, allowed, kept_values):
    (
        normed_self,
        inverse_self,
        whole_self,
        self_parts,
        attended,
        self_log,
        normed_cross,
        inverse_cross,
        whole_cross,
        cross_query,
        text_heads,
        cross_out,
        cross_log,
        normed_mlp,
        inverse_mlp,
        whole_mlp,
        hidden,
        active,
    ) = kept_values
    gain_w = weights[1].astype(jnp.float32)
    col_w = weights[2][layer_index]
    row_w = weights[4][layer_index]
    items, frames = (whole_self.shape[0], whole_self.shape[1])
    head_count = col_w.shape[-1] // HEAD_DIM
    score_scale = HEAD_DIM ** (-0.5)
    branch_grad = gather_grads(resid_grad)
    active_grad = jnp.einsum(
        "ifd,sdc->ifsc", branch_grad, row_w[2:6], preferred_element_type=jnp.float32
    )
    row_mlp = jnp.einsum("ifsc,ifd->sdc", active, branch_grad, preferred_element_type=jnp.float32)
    hidden_grad = as_low(jax.vjp(gelu_tanh, hidden)[1](active_grad)[0])
    col_mlp = jnp.einsum(
        "ifd,ifsc->dsc", whole_mlp, hidden_grad, preferred_element_type=jnp.float32
    )
    input_grad = sum_grads(
        jnp.einsum("ifsc,dsc->ifd", hidden_grad, col_w[:, 4:8], preferred_element_type=jnp.float32)
    )
    step_grad, gain_mlp = norm_back(
        input_grad, gain_w[3 * layer_index + 2], normed_mlp, inverse_mlp
    )
    resid_grad = resid_grad + step_grad
    branch_grad = gather_grads(resid_grad)
    cross_grad = as_low(
        jnp.einsum("ifd,dc->ifc", branch_grad, row_w[1], preferred_element_type=jnp.float32)
    )
    row_cross = jnp.einsum(
        "ifc,ifd->dc", cross_out, branch_grad, preferred_element_type=jnp.float32
    )
    query_grad, key_grad, value_grad = attend_backward(
        cross_query.reshape(items, frames, head_count, HEAD_DIM),
        text_heads[:, :, 0],
        text_heads[:, :, 1],
        allowed,
        score_scale,
        cross_log,
        cross_grad.reshape(items, frames, head_count, HEAD_DIM),
    )
    query_low = as_low(query_grad.reshape(items, frames, -1))
    text_grad = as_low(
        jnp.stack([key_grad, value_grad], 2).reshape(items, text_feat.shape[1], 2, -1)
    )
    kv_grad = jnp.einsum("itd,itsc->dsc", text_feat, text_grad, preferred_element_type=jnp.float32)
    col_cross = jnp.einsum(
        "ifd,ifc->dc", whole_cross, query_low, preferred_element_type=jnp.float32
    )
    input_grad = sum_grads(
        jnp.einsum("ifc,dc->ifd", query_low, col_w[:, 3], preferred_element_type=jnp.float32)
    )
    step_grad, gain_cross = norm_back(
        input_grad, gain_w[3 * layer_index + 1], normed_cross, inverse_cross
    )
    resid_grad = resid_grad + step_grad
    branch_grad = gather_grads(resid_grad)
    self_grad = as_low(
        jnp.einsum("ifd,dc->ifc", branch_grad, row_w[0], preferred_element_type=jnp.float32)
    )
    row_self = jnp.einsum("ifc,ifd->dc", attended, branch_grad, preferred_element_type=jnp.float32)
    self_query, self_keys, self_values = self_parts
    query_grad, key_grad, value_grad = attend_backward(
        self_query,
        self_keys,
        self_values,
        jnp.ones((items, self_keys.shape[1]), bool),
        score_scale,
        self_log,
        self_grad.reshape(items, frames, head_count, HEAD_DIM),
    )
    proj_grad = as_low(
        jnp.stack([query_grad, key_grad, value_grad], 2).reshape(items, frames, 3, -1)
    )
    col_self = jnp.einsum(
        "ifd,ifsc->dsc", whole_self, proj_grad, preferred_element_type=jnp.float32
    )
    input_grad = sum_grads(
        jnp.einsum("ifsc,dsc->ifd", proj_grad, col_w[:, 0:3], preferred_element_type=jnp.float32)
    )
    step_grad, gain_self = norm_back(input_grad, gain_w[3 * layer_index], normed_self, inverse_self)
    resid_grad = resid_grad + step_grad
    col_grad = jnp.concatenate([col_self, col_cross[:, None], col_mlp], 1)
    row_grad = jnp.concatenate([row_self[None], row_cross[None], row_mlp], 0)
    return (resid_grad, (col_grad, kv_grad, row_grad, jnp.stack([gain_self, gain_cross, gain_mlp])))


def adam_update(master, first_moment, second_moment, average, gradient, factor, step_rate):
    clipped = gradient * factor
    first_new = beta_first * first_moment + (1.0 - beta_first) * clipped
    second_new = beta_second * second_moment + (1.0 - beta_second) * clipped * clipped
    first_hat = first_new / (1.0 - beta_first**STEP)
    second_hat = second_new / (1.0 - beta_second**STEP)
    master_new = master - step_rate * (
        first_hat / (jnp.sqrt(second_hat) + adam_eps) + weight_decay * master
    )
    return (
        master_new,
        first_new,
        second_new,
        average_keep * average + (1.0 - average_keep) * master_new,
    )


def local(
    latents,
    noise_draw,
    timesteps,
    text_ids,
    text_len,
    item_counts,
    text_table,
    io_weight,
    io_first,
    io_second,
    io_average,
    norm_gains,
    gains_first,
    gains_second,
    gains_average,
    col_weight,
    col_first,
    col_second,
    col_average,
    text_weight,
    text_first,
    text_second,
    text_average,
    row_weight,
    row_first,
    row_second,
    row_average,
):
    weights = (
        lax.all_gather(as_low(io_weight), "dp", axis=2, tiled=True),
        lax.all_gather(as_low(norm_gains), "dp", axis=1, tiled=True),
        lax.all_gather(as_low(col_weight), "dp", axis=1, tiled=True),
        lax.all_gather(as_low(text_weight), "dp", axis=1, tiled=True),
        lax.all_gather(as_low(row_weight), "dp", axis=2, tiled=True),
    )
    item_total = lax.psum(jnp.sum(item_counts).astype(jnp.float32), "dp")
    table_rows = text_table.shape[0]
    local_ids = text_ids - lax.axis_index("mp") * table_rows
    inside = (local_ids >= 0) & (local_ids < table_rows)
    picked = text_table[jnp.clip(local_ids, 0, table_rows - 1)].astype(jnp.float32)
    picked = jnp.where(inside[..., None], picked, 0.0)
    text_feat = as_low(lax.psum(picked.astype(jnp.bfloat16), "mp").astype(jnp.float32))
    allowed = jnp.arange(text_ids.shape[1])[None, :] < text_len[:, None]
    items, channels, frame_part = latents.shape
    levels = weights[2].shape[0]
    model_width = weights[1].shape[1]
    io_w = weights[0]
    gain_w = weights[1].astype(jnp.float32)
    alpha_bar = jnp.sum(
        jnp.where(timesteps[:, None] == jnp.arange(1000)[None, :], plan()[None, :], 0.0), -1
    )
    noisy = (
        jnp.sqrt(alpha_bar)[:, None, None] * latents
        + jnp.sqrt(1.0 - alpha_bar)[:, None, None] * noise_draw
    )
    noisy_low = as_low(noisy)
    frame_pos = (lax.axis_index("mp") * frame_part + jnp.arange(frame_part)).astype(jnp.float32)
    resid = jnp.einsum("icf,cd->ifd", noisy_low, io_w[0], preferred_element_type=jnp.float32)
    resid = (
        resid
        + sinusoid(frame_pos, model_width)[None]
        + sinusoid(timesteps.astype(jnp.float32), model_width)[:, None]
    )
    kept_all = []
    for layer_index in range(levels):
        resid, kept_values = layer_forward(resid, weights, layer_index, text_feat, allowed)
        kept_all.append(kept_values)
    final_out, final_normed, final_inverse = layer_norm(resid, gain_w[3 * levels])
    final_low = as_low(final_out)
    predicted = jnp.einsum("ifd,cd->icf", final_low, io_w[1], preferred_element_type=jnp.float32)
    residual_error = predicted - noise_draw
    snr_ratio = alpha_bar / (1.0 - alpha_bar)
    loss_weight = jnp.minimum(snr_ratio, snr_limit) / snr_ratio
    valid_items = (jnp.arange(items) < item_counts[0]).astype(jnp.float32)
    item_scale = valid_items * loss_weight / (channels * frame_part * lax.axis_size("mp"))
    loss_part = jnp.sum(item_scale * jnp.sum(residual_error * residual_error, axis=(1, 2)))
    pred_grad = as_low((2.0 * item_scale / item_total)[:, None, None] * residual_error)
    out_proj_grad = jnp.einsum(
        "icf,ifd->cd", pred_grad, final_low, preferred_element_type=jnp.float32
    )
    final_grad = jnp.einsum("icf,cd->ifd", pred_grad, io_w[1], preferred_element_type=jnp.float32)
    resid_grad, gain_final = norm_back(final_grad, gain_w[3 * levels], final_normed, final_inverse)
    pieces = [None] * levels
    for layer_index in reversed(range(levels)):
        resid_grad, layer_grads = layer_backward(
            resid_grad, weights, layer_index, text_feat, allowed, kept_all[layer_index]
        )
        pieces[layer_index] = layer_grads
    in_proj_grad = jnp.einsum(
        "icf,ifd->cd", noisy_low, as_low(resid_grad), preferred_element_type=jnp.float32
    )
    io_grad = jnp.stack([in_proj_grad, out_proj_grad])
    gain_grad = jnp.concatenate([piece[3] for piece in pieces] + [gain_final[None]], 0)
    col_grad = jnp.stack([piece[0] for piece in pieces])
    kv_grad = jnp.stack([piece[1] for piece in pieces])
    row_grad = jnp.stack([piece[2] for piece in pieces])
    io_grad, gain_grad, col_grad, kv_grad, row_grad = (
        lax.psum_scatter(
            io_grad.astype(jnp.bfloat16), "dp", scatter_dimension=2, tiled=True
        ).astype(jnp.float32),
        lax.psum_scatter(
            gain_grad.astype(jnp.bfloat16), "dp", scatter_dimension=1, tiled=True
        ).astype(jnp.float32),
        lax.psum_scatter(
            col_grad.astype(jnp.bfloat16), "dp", scatter_dimension=1, tiled=True
        ).astype(jnp.float32),
        lax.psum_scatter(
            kv_grad.astype(jnp.bfloat16), "dp", scatter_dimension=1, tiled=True
        ).astype(jnp.float32),
        lax.psum_scatter(
            row_grad.astype(jnp.bfloat16), "dp", scatter_dimension=2, tiled=True
        ).astype(jnp.float32),
    )
    io_grad, gain_grad = lax.psum((io_grad, gain_grad), "mp")
    owner_mask = (lax.axis_index("mp") == 0).astype(jnp.float32)
    square = (
        jnp.sum(col_grad * col_grad) + jnp.sum(kv_grad * kv_grad) + jnp.sum(row_grad * row_grad)
    )
    square = square + owner_mask * (jnp.sum(io_grad * io_grad) + jnp.sum(gain_grad * gain_grad))
    totals = lax.psum((square, loss_part), ("dp", "mp"))
    grad_norm = jnp.sqrt(totals[0])
    factor = jnp.minimum(1.0, clip_limit / (grad_norm + 1e-06))
    results = [totals[1], item_total, grad_norm]
    io_updated = adam_update(
        io_weight, io_first, io_second, io_average, io_grad, factor, matrix_rate
    )
    results.extend(
        [io_updated[0], io_updated[1], io_updated[2][0], io_updated[2][1], io_updated[3]]
    )
    results.extend(
        adam_update(
            norm_gains, gains_first, gains_second, gains_average, gain_grad, factor, gain_rate
        )
    )
    results.extend(
        adam_update(col_weight, col_first, col_second, col_average, col_grad, factor, matrix_rate)
    )
    results.extend(
        adam_update(
            text_weight, text_first, text_second, text_average, kv_grad, factor, matrix_rate
        )
    )
    results.extend(
        adam_update(row_weight, row_first, row_second, row_average, row_grad, factor, row_rate)
    )
    return tuple(results)


def solution(mesh):
    return jax.shard_map(
        local,
        mesh=mesh,
        in_specs=(
            P("dp", None, "mp"),
            P("dp", None, "mp"),
            P("dp"),
            P("dp", None),
            P("dp"),
            P("dp"),
            P("mp", None),
            P(None, None, "dp"),
            P(None, None, "dp"),
            P(None, None, "dp"),
            P(None, None, "dp"),
            P(None, "dp"),
            P(None, "dp"),
            P(None, "dp"),
            P(None, "dp"),
            P(None, "dp", None, "mp"),
            P(None, "dp", None, "mp"),
            P(None, "dp", None, "mp"),
            P(None, "dp", None, "mp"),
            P(None, "dp", None, "mp"),
            P(None, "dp", None, "mp"),
            P(None, "dp", None, "mp"),
            P(None, "dp", None, "mp"),
            P(None, None, "dp", "mp"),
            P(None, None, "dp", "mp"),
            P(None, None, "dp", "mp"),
            P(None, None, "dp", "mp"),
        ),
        out_specs=(
            P(),
            P(),
            P(),
            P(None, None, "dp"),
            P(None, None, "dp"),
            P(None, "dp"),
            P(None, "dp"),
            P(None, None, "dp"),
            P(None, "dp"),
            P(None, "dp"),
            P(None, "dp"),
            P(None, "dp"),
            P(None, "dp", None, "mp"),
            P(None, "dp", None, "mp"),
            P(None, "dp", None, "mp"),
            P(None, "dp", None, "mp"),
            P(None, "dp", None, "mp"),
            P(None, "dp", None, "mp"),
            P(None, "dp", None, "mp"),
            P(None, "dp", None, "mp"),
            P(None, None, "dp", "mp"),
            P(None, None, "dp", "mp"),
            P(None, None, "dp", "mp"),
            P(None, None, "dp", "mp"),
        ),
        check_vma=False,
    )
```

profile of v0, /device:TPU:0, one launch (start us, length us, event | category | flops | bytes accessed | tf_op | source)
XLA Modules:
  0.0 2346.1 jit_solution(11221352103142632)
XLA Ops:
  89.2 51.7 %all-gather.18.cloned.1.call-done = bf16[2,1024,8,256]{1,3,2,0:T(8,128)(2,1)} async-done(((bf16[2,128,8,256]{1,3,2,0:T(8,128)(2,1)}), bf16[2,1024,8,256]{1,3,2,0:T(8,128)(2,1)}) %all-gather.18.cloned.1.call-update) | async-done | bytes 8388624 | tf_op jit(solution)/shard_map/all_gather | solution.py:385
  214.8 62.0 %all-gather.20.cloned.1.call-done = bf16[2,6,1024,256]{3,2,1,0:T(8,128)(2,1)} async-done(((bf16[2,6,128,256]{3,2,1,0:T(8,128)(2,1)}), bf16[2,6,1024,256]{3,2,1,0:T(8,128)(2,1)}) %all-gather.20.cloned.1.call-update) | async-done | bytes 6291472 | tf_op jit(solution)/shard_map/all_gather | solution.py:387
  359.9 46.8 %all-gather.24.cloned.1.call-done = bf16[2,768,2,256]{3,1,2,0:T(8,128)(2,1)} async-done(((bf16[2,96,2,256]{3,1,2,0:T(8,128)(2,1)}), bf16[2,768,2,256]{3,1,2,0:T(8,128)(2,1)}) %all-gather.24.cloned.1.call-update) | async-done | bytes 1572880 | tf_op jit(solution)/shard_map/all_gather | solution.py:386
  469.6 44.6 %reduce-scatter.24.cloned.1.call-done = bf16[2,256,1024]{2,1,0:T(8,128)(2,1)} async-done(((bf16[2,1024,1024]{2,1,0:T(8,128)(2,1)}), bf16[2,256,1024]{2,1,0:T(8,128)(2,1)}) %reduce-scatter.24.cloned.1.call-update) | async-done | bytes 1048592 | tf_op jit(solution)/shard_map/reduce_scatter | solution.py:67
  571.6 44.6 %reduce-scatter.26.cloned.1.call-done = bf16[2,256,1024]{2,1,0:T(8,128)(2,1)} async-done(((bf16[2,1024,1024]{2,1,0:T(8,128)(2,1)}), bf16[2,256,1024]{2,1,0:T(8,128)(2,1)}) %reduce-scatter.26.cloned.1.call-update) | async-done | bytes 1048592 | tf_op jit(solution)/shard_map/reduce_scatter | solution.py:67
  620.4 34.6 %all-gather.28.cloned.1.call-done = bf16[2,1024,1024]{2,1,0:T(8,128)(2,1)} async-done(((bf16[2,256,1024]{2,1,0:T(8,128)(2,1)}), bf16[2,1024,1024]{2,1,0:T(8,128)(2,1)}) %all-gather.28.cloned.1.call-update) | async-done | bytes 4194320 | tf_op jit(solution)/shard_map/all_gather | solution.py:63
  695.9 44.4 %reduce-scatter.28.cloned.1.call-done = bf16[2,256,1024]{2,1,0:T(8,128)(2,1)} async-done(((bf16[2,1024,1024]{2,1,0:T(8,128)(2,1)}), bf16[2,256,1024]{2,1,0:T(8,128)(2,1)}) %reduce-scatter.28.cloned.1.call-update) | async-done | bytes 1048592 | tf_op jit(solution)/shard_map/reduce_scatter | solution.py:67
  805.9 44.6 %reduce-scatter.30.cloned.1.call-done = bf16[2,256,1024]{2,1,0:T(8,128)(2,1)} async-done(((bf16[2,1024,1024]{2,1,0:T(8,128)(2,1)}), bf16[2,256,1024]{2,1,0:T(8,128)(2,1)}) %reduce-scatter.30.cloned.1.call-update) | async-done | bytes 1048592 | tf_op jit(solution)/shard_map/reduce_scatter | solution.py:67
  907.9 44.6 %reduce-scatter.32.cloned.1.call-done = bf16[2,256,1024]{2,1,0:T(8,128)(2,1)} async-done(((bf16[2,1024,1024]{2,1,0:T(8,128)(2,1)}), bf16[2,256,1024]{2,1,0:T(8,128)(2,1)}) %reduce-scatter.32.cloned.1.call-update) | async-done | bytes 1048592 | tf_op jit(solution)/shard_map/reduce_scatter | solution.py:67
  1017.6 44.6 %reduce-scatter.34.cloned.1.call-done = bf16[2,256,1024]{2,1,0:T(8,128)(2,1)} async-done(((bf16[2,1024,1024]{2,1,0:T(8,128)(2,1)}), bf16[2,256,1024]{2,1,0:T(8,128)(2,1)}) %reduce-scatter.34.cloned.1.call-update) | async-done | bytes 1048592 | tf_op jit(solution)/shard_map/reduce_scatter | solution.py:77
  1143.7 44.5 %reduce-scatter.36.cloned.1.call-done = bf16[2,256,1024]{2,1,0:T(8,128)(2,1)} async-done(((bf16[2,1024,1024]{2,1,0:T(8,128)(2,1)}), bf16[2,256,1024]{2,1,0:T(8,128)(2,1)}) %reduce-scatter.36.cloned.1.call-update) | async-done | bytes 1048592 | tf_op jit(solution)/shard_map/reduce_scatter | solution.py:77
  1197.7 34.6 %all-gather.38.cloned.1.call-done = bf16[2,1024,1024]{2,1,0:T(8,128)(2,1)} async-done(((bf16[2,256,1024]{2,1,0:T(8,128)(2,1)}), bf16[2,1024,1024]{2,1,0:T(8,128)(2,1)}) %all-gather.38.cloned.1.call-update) | async-done | bytes 4194320 | tf_op jit(solution)/shard_map/all_gather | solution.py:73
  1239.7 80.4 %while.115 = (s32[]{:T(128)}, f32[2,1024,4,64]{1,3,2,0:T(8,128)}, f32[2,1024,4,64]{1,3,2,0:T(8,128)}, bf16[2,2,512,4,64]{2,4,3,1,0:T(8,128)(2,1)}, bf16[2,2,512,...) while((s32[]{:T(128)}, f32[2,1024,4,64]{1,3,2,0:T(8,128)}, ...), condition=%wide.region_57.58_spmd.clone, body=%wide.region_55.57_spmd.clone.sunk | while | flops 2737565696 | bytes 190955760 | solution.py:147
  1340.8 44.6 %reduce-scatter.38.cloned.1.call-done = bf16[2,256,1024]{2,1,0:T(8,128)(2,1)} async-done(((bf16[2,1024,1024]{2,1,0:T(8,128)(2,1)}), bf16[2,256,1024]{2,1,0:T(8,128)(2,1)}) %reduce-scatter.38.cloned.1.call-update) | async-done | bytes 1048592 | tf_op jit(solution)/shard_map/reduce_scatter | solution.py:77
  1447.4 44.6 %reduce-scatter.40.cloned.1.call-done = bf16[2,256,1024]{2,1,0:T(8,128)(2,1)} async-done(((bf16[2,1024,1024]{2,1,0:T(8,128)(2,1)}), bf16[2,256,1024]{2,1,0:T(8,128)(2,1)}) %reduce-scatter.40.cloned.1.call-update) | async-done | bytes 1048592 | tf_op jit(solution)/shard_map/reduce_scatter | solution.py:77
  1499.8 34.6 %all-gather.42.cloned.1.call-done = bf16[2,1024,1024]{2,1,0:T(8,128)(2,1)} async-done(((bf16[2,256,1024]{2,1,0:T(8,128)(2,1)}), bf16[2,1024,1024]{2,1,0:T(8,128)(2,1)}) %all-gather.42.cloned.1.call-update) | async-done | bytes 4194320 | tf_op jit(solution)/shard_map/all_gather | solution.py:73
  1560.0 44.6 %reduce-scatter.42.cloned.1.call-done = bf16[2,256,1024]{2,1,0:T(8,128)(2,1)} async-done(((bf16[2,1024,1024]{2,1,0:T(8,128)(2,1)}), bf16[2,256,1024]{2,1,0:T(8,128)(2,1)}) %reduce-scatter.42.cloned.1.call-update) | async-done | bytes 1048592 | tf_op jit(solution)/shard_map/reduce_scatter | solution.py:77
  1610.0 34.6 %all-gather.44.cloned.1.call-done = bf16[2,1024,1024]{2,1,0:T(8,128)(2,1)} async-done(((bf16[2,256,1024]{2,1,0:T(8,128)(2,1)}), bf16[2,1024,1024]{2,1,0:T(8,128)(2,1)}) %all-gather.44.cloned.1.call-update) | async-done | bytes 4194320 | tf_op jit(solution)/shard_map/all_gather | solution.py:73
  1654.1 75.1 %while.117 = (s32[]{:T(128)}, f32[2,1024,4,64]{1,3,2,0:T(8,128)}, f32[2,1024,4,64]{1,3,2,0:T(8,128)}, bf16[2,2,512,4,64]{2,4,3,1,0:T(8,128)(2,1)}, bf16[2,2,512,...) while((s32[]{:T(128)}, f32[2,1024,4,64]{1,3,2,0:T(8,128)}, ...), condition=%wide.region_72.73_spmd.clone, body=%wide.region_70.72_spmd.clone.sunk | while | flops 2737565696 | bytes 195150096 | solution.py:147
  1866.0 62.2 %reduce-scatter.54.cloned.1.call-done = bf16[128,7]{1,0:T(8,128)(2,1)} async-done(((bf16[1024,7]{1,0:T(8,128)(2,1)}), bf16[128,7]{1,0:T(8,128)(2,1)}) %reduce-scatter.54.cloned.1.call-update) | async-done | bytes 1808
  1929.1 63.4 %reduce-scatter.52.cloned.1.call-done = bf16[128,40]{1,0:T(8,128)(2,1)} async-done(((bf16[1024,40]{1,0:T(8,128)(2,1)}), bf16[128,40]{1,0:T(8,128)(2,1)}) %reduce-scatter.52.cloned.1.call-update) | async-done | bytes 10256
  2006.2 107.3 %reduce-scatter.48.cloned.1.call-done = bf16[2,6,128,256]{3,2,1,0:T(8,128)(2,1)} async-done(((bf16[2,6,1024,256]{3,2,1,0:T(8,128)(2,1)}), bf16[2,6,128,256]{3,2,1,0:T(8,128)(2,1)}) %reduce-scatter.48.cloned.1.call-update) | async-done | bytes 786448 | tf_op jit(solution)/shard_map/reduce_scatter | solution.py:463
  2115.6 149.9 %reduce-scatter.44.cloned.1.call-done = bf16[2,128,8,256]{3,1,2,0:T(8,128)(2,1)} async-done(((bf16[2,1024,8,256]{3,1,2,0:T(8,128)(2,1)}), bf16[2,128,8,256]{3,1,2,0:T(8,128)(2,1)}) %reduce-scatter.44.cloned.1.call-update) | async-done | bytes 1048592 | tf_op jit(solution)/shard_map/reduce_scatter | solution.py:457
  2269.8 39.5 %all-reduce.1 = (f32[]{:T(128)}, f32[]{:T(128)}) all-reduce(f32[]{:T(128)} %multiply_reduce_fusion.19, f32[]{:T(128)S(6)} %add.447), channel_id=1, replica_groups=mesh['dp'=8,'mp'=4] {'dp','mp'}, use_global_device_ids=true, to_apply=%region_42.43 | all-reduce | flops 2 | bytes 16 | tf_op jit(solution)/shard_map/psum | solution.py:473
  (921 shorter events, 1240.0 us)
Async XLA Ops:
  7.2 133.6 %all-gather.18.cloned.1.call-start = ((), (), s32[]{:S(2)}) async-start(), calls=%async_computation.18 | async-start | bytes 9437184 | tf_op jit(solution)/shard_map/all_gather | solution.py:385
  10.0 165.0 %all-gather.16.cloned.1.call-start = ((), (), s32[]{:S(2)}) async-start(), calls=%async_computation.17 | async-start | bytes 5242880 | tf_op jit(solution)/shard_map/all_gather | solution.py:63
  87.2 189.6 %all-gather.20.cloned.1.call-start = ((), (), s32[]{:S(2)}) async-start(), calls=%async_computation.19 | async-start | bytes 7077888 | tf_op jit(solution)/shard_map/all_gather | solution.py:387
  88.7 235.7 %reduce-scatter.22.cloned.1.call-start = ((), (), s32[]{:S(2)}) async-start(), calls=%async_computation.20 | async-start | bytes 5242880 | tf_op jit(solution)/shard_map/reduce_scatter | solution.py:67
  291.4 115.4 %all-gather.24.cloned.1.call-start = ((), (), s32[]{:S(2)}) async-start(), calls=%async_computation.23 | async-start | bytes 1769472 | tf_op jit(solution)/shard_map/all_gather | solution.py:386
  292.2 150.1 %all-gather.22.cloned.1.call-start = ((), (), s32[]{:S(2)}) async-start(), calls=%async_computation.21 | async-start | bytes 5242880 | tf_op jit(solution)/shard_map/all_gather | solution.py:63
  329.1 185.1 %reduce-scatter.24.cloned.1.call-start = ((), (), s32[]{:S(2)}) async-start(), calls=%async_computation.24 | async-start | bytes 5242880 | tf_op jit(solution)/shard_map/reduce_scatter | solution.py:67
  518.4 97.8 %reduce-scatter.26.cloned.1.call-start = ((), (), s32[]{:S(2)}) async-start(), calls=%async_computation.26 | async-start | bytes 5242880 | tf_op jit(solution)/shard_map/reduce_scatter | solution.py:67
  620.3 120.0 %reduce-scatter.28.cloned.1.call-start = ((), (), s32[]{:S(2)}) async-start(), calls=%async_computation.28 | async-start | bytes 5242880 | tf_op jit(solution)/shard_map/reduce_scatter | solution.py:67
  744.5 106.0 %reduce-scatter.30.cloned.1.call-start = ((), (), s32[]{:S(2)}) async-start(), calls=%async_computation.30 | async-start | bytes 5242880 | tf_op jit(solution)/shard_map/reduce_scatter | solution.py:67
  854.8 97.7 %reduce-scatter.32.cloned.1.call-start = ((), (), s32[]{:S(2)}) async-start(), calls=%async_computation.32 | async-start | bytes 5242880 | tf_op jit(solution)/shard_map/reduce_scatter | solution.py:67
  907.9 87.7 %all-gather.34.cloned.1.call-start = ((), (), s32[]{:S(2)}) async-start(), calls=%async_computation.33 | async-start | bytes 5242880 | tf_op jit(solution)/shard_map/all_gather | solution.py:73
  960.9 101.3 %reduce-scatter.34.cloned.1.call-start = ((), (), s32[]{:S(2)}) async-start(), calls=%async_computation.34 | async-start | bytes 5242880 | tf_op jit(solution)/shard_map/reduce_scatter | solution.py:77
  1068.7 119.5 %reduce-scatter.36.cloned.1.call-start = ((), (), s32[]{:S(2)}) async-start(), calls=%async_computation.36 | async-start | bytes 5242880 | tf_op jit(solution)/shard_map/reduce_scatter | solution.py:77
  1143.7 88.6 %all-gather.38.cloned.1.call-start = ((), (), s32[]{:S(2)}) async-start(), calls=%async_computation.37 | async-start | bytes 5242880 | tf_op jit(solution)/shard_map/all_gather | solution.py:73
  1197.7 187.8 %reduce-scatter.38.cloned.1.call-start = ((), (), s32[]{:S(2)}) async-start(), calls=%async_computation.38 | async-start | bytes 5242880 | tf_op jit(solution)/shard_map/reduce_scatter | solution.py:77
  1390.2 101.8 %reduce-scatter.40.cloned.1.call-start = ((), (), s32[]{:S(2)}) async-start(), calls=%async_computation.40 | async-start | bytes 5242880 | tf_op jit(solution)/shard_map/reduce_scatter | solution.py:77
  1499.7 104.9 %reduce-scatter.42.cloned.1.call-start = ((), (), s32[]{:S(2)}) async-start(), calls=%async_computation.42 | async-start | bytes 5242880 | tf_op jit(solution)/shard_map/reduce_scatter | solution.py:77
  1610.0 185.7 %reduce-scatter.50.cloned.1.call-start = ((), (), s32[]{:S(2)}) async-start(), calls=%async_computation.47 | async-start | bytes 5242880 | tf_op jit(solution)/shard_map/reduce_scatter | solution.py:77
  1750.3 114.0 %reduce-scatter.46.cloned.1.call-start = ((), (), s32[]{:S(2)}) async-start(), calls=%async_computation.45 | async-start | bytes 1769472 | tf_op jit(solution)/shard_map/reduce_scatter | solution.py:460
  1779.6 148.6 %reduce-scatter.54.cloned.1.call-start = ((), (), s32[]{:S(2)}) async-start(), calls=%async_computation.49 | async-start | bytes 294912
  1799.8 192.6 %reduce-scatter.52.cloned.1.call-start = ((), (), s32[]{:S(2)}) async-start(), calls=%async_computation.48 | async-start | bytes 294912
  1804.8 308.6 %reduce-scatter.48.cloned.1.call-start = ((), (), s32[]{:S(2)}) async-start(), calls=%async_computation.46 | async-start | bytes 7077888 | tf_op jit(solution)/shard_map/reduce_scatter | solution.py:463
  1811.1 454.4 %reduce-scatter.44.cloned.1.call-start = ((), (), s32[]{:S(2)}) async-start(), calls=%async_computation.44 | async-start | bytes 9437184 | tf_op jit(solution)/shard_map/reduce_scatter | solution.py:457
  (248 other events, 6583.9 us)
Sparse Core Ops, SparseCore 0:
  10.7 130.1 all-gather.17
  177.8 99.0 all-gather.19
  281.7 42.6 reduce-scatter.21
  362.6 44.1 all-gather.23
  469.7 44.4 reduce-scatter.23
  571.6 44.5 reduce-scatter.25
  620.5 34.4 all-gather.27
  695.8 44.4 reduce-scatter.27
  806.0 44.5 reduce-scatter.29
  854.9 34.4 all-gather.31
  908.0 44.4 reduce-scatter.31
  1017.6 44.5 reduce-scatter.33
  1068.9 34.4 all-gather.35
  1143.7 44.4 reduce-scatter.35
  1340.9 44.5 reduce-scatter.37
  1447.5 44.4 reduce-scatter.39
  1560.0 44.5 reduce-scatter.41
  1610.1 34.4 all-gather.43
  1750.4 44.4 reduce-scatter.49
  1799.4 64.8 reduce-scatter.45
  1868.0 60.1 reduce-scatter.53
  1932.1 60.2 reduce-scatter.51
  1996.0 117.3 reduce-scatter.47
  2116.9 148.5 reduce-scatter.43
  (9 shorter events, 304.2 us)
where the time goes:
time: 2350 us
  waiting for transfers between devices  1470 us (63%)
  matrix products  372 us (16%)
  local copies, waits for them, and re-layouts  188 us (8%)
  other arithmetic  171 us (7%)
  blocking collectives  117 us (5%)
    reduce_scatter x6, waiting for transfers between devices, sum_rows(): lax.psum_scatter(tensor.astype(jnp.bfloat16), 'mp', scatter_dimension=1,...  255 us
    reduce_scatter x6, waiting for transfers between devices, sum_grads(): lax.psum_scatter(tensor.astype(jnp.bfloat16), 'mp', scatter_dimension=1,...  223 us
    all_gather x6, waiting for transfers between devices, gather_grads(): return lax.all_gather(as_low(tensor), 'mp', axis=1, tiled=True)  207 us
    all_gather x6, waiting for transfers between devices, gather_rows(): return lax.all_gather(tensor, 'mp', axis=1, tiled=True)  198 us
    reduce_scatter x1, waiting for transfers between devices, local(): lax.psum_scatter(col_grad.astype(jnp.bfloat16), 'dp', scatter_dimension=1...  150 us
    unnamed x35, waiting for transfers between devices  126 us
    reduce_scatter x1, waiting for transfers between devices, local(): lax.psum_scatter(row_grad.astype(jnp.bfloat16), 'dp', scatter_dimension=2...  107 us
    convert_element_type x24, other arithmetic, as_low(): return tensor.astype(jnp.bfloat16)  71.3 us
  transfers between devices with their start and end apart: 33, of which 32 were waited for; matrix products, arithmetic and copies ran while one was open for 7% of the time, Pallas kernels for 0%

commit v1 on v0

v1 whole, which is shorter than its diff:
```python
import functools
import math

import jax
import jax.numpy as jnp
from jax import lax
from jax.experimental import pallas as pl
from jax.experimental.pallas import tpu as pltpu
from jax.sharding import PartitionSpec as P

HEAD_DIM = 64
STEP = 10
LANES = 128

norm_eps = 1e-06
clip_limit = 0.001
matrix_rate = 0.04
gain_rate = 0.6
row_rate = 0.1
beta_first = 0.9
beta_second = 0.999
adam_eps = 1e-08
weight_decay = 0.01
average_keep = 0.5
snr_limit = 5.0

score_scale = HEAD_DIM ** (-0.5)
log2_e = 1.4426950408889634
exp_scale = score_scale * log2_e
masked_score = -1e30


def as_low(tensor):
    return tensor.astype(jnp.bfloat16)


def plan():
    beta_table = jnp.linspace(0.00085**0.5, 0.012**0.5, 1000, dtype=jnp.float32) ** 2
    return jnp.cumprod(1.0 - beta_table)


def exchange(tensor, axis, mask):
    size = lax.axis_size(axis)
    return lax.ppermute(tensor, axis, [(i, i ^ mask) for i in range(size)])


class Layout:
    def __init__(self, items):
        self.dp_size = lax.axis_size("dp")
        self.mp_size = lax.axis_size("mp")
        self.ranks = self.mp_size // items
        self.item = lax.axis_index("mp") // self.ranks
        self.rank = lax.axis_index("mp") % self.ranks
        self.dp = lax.axis_index("dp")
        self.masks = []
        mask = self.dp_size >> 1
        while mask:
            self.masks.append(mask)
            mask >>= 1
        self.offsets = [
            sum(mask for bit, mask in enumerate(self.masks) if (place >> bit) & 1)
            for place in range(self.dp_size)
        ]

    def blocks(self):
        return jnp.bitwise_xor(self.dp, jnp.array(self.offsets, jnp.int32))

    def other_item(self, tensor):
        return exchange(tensor, "mp", self.ranks)

    def rank_pair(self, tensor):
        mask = 1
        while mask * 2 < self.ranks:
            tensor = as_low(
                tensor.astype(jnp.float32) + exchange(tensor, "mp", mask).astype(jnp.float32)
            )
            mask *= 2
        return (tensor, exchange(tensor, "mp", mask))


def gather_dp(layout, part, axis, masks):
    for mask in masks:
        part = jnp.concatenate([part, exchange(part, "dp", mask)], axis)
    return part


def gather_last_item(layout, part, axis):
    part = gather_dp(layout, part, axis, layout.masks)
    return [part, layout.other_item(part)]


def gather_last_dp(layout, part, axis):
    part = gather_dp(layout, part, axis, layout.masks[:-1])
    pair = [part, layout.other_item(part)]
    return [gather_dp(layout, half, axis, layout.masks[-1:]) for half in pair]


def add_terms(terms):
    total = terms[0].astype(jnp.float32)
    for term in terms[1:]:
        total = total + term.astype(jnp.float32)
    return total


def halve(layout, terms, mask, kind):
    half = terms[0].shape[0] // 2
    send = add_terms([term[half:] for term in terms]).astype(kind)
    return [term[:half] for term in terms] + [exchange(send, "dp", mask)]


def scatter_first_item(layout, pair):
    kind = pair[0].dtype
    terms = [pair[0], layout.other_item(pair[1])]
    for mask in reversed(layout.masks):
        terms = halve(layout, terms, mask, kind)
    return add_terms(terms)


def scatter_first_dp(layout, pair):
    kind = pair[0].dtype
    mine, theirs = [halve(layout, [part], layout.masks[-1], kind) for part in pair]
    terms = mine + [layout.other_item(add_terms(theirs).astype(kind))]
    for mask in reversed(layout.masks[:-1]):
        terms = halve(layout, terms, mask, kind)
    return add_terms(terms)


def norm_forward_kernel(parts, *refs):
    resid_ref, gain_ref = refs[0], refs[1]
    resid = resid_ref[...]
    if parts:
        resid = resid + (refs[2][...].astype(jnp.float32) + refs[3][...].astype(jnp.float32))
        refs[4][...] = resid
    centre = resid - jnp.mean(resid, -1, keepdims=True)
    inverse = lax.rsqrt(jnp.mean(centre * centre, -1, keepdims=True) + norm_eps)
    refs[-1][...] = (centre * inverse * gain_ref[...]).astype(jnp.bfloat16)


def norm_forward(resid, gain, parts=()):
    frames, width = resid.shape
    rows = min(256, frames)
    block = pl.BlockSpec((rows, width), lambda i: (i, 0))
    low_shape = jax.ShapeDtypeStruct((frames, width), jnp.bfloat16)
    result = pl.pallas_call(
        functools.partial(norm_forward_kernel, len(parts)),
        grid=(frames // rows,),
        in_specs=[block, pl.BlockSpec((1, width), lambda i: (0, 0))] + [block] * len(parts),
        out_specs=[block, block] if parts else [block],
        out_shape=[jax.ShapeDtypeStruct((frames, width), jnp.float32), low_shape]
        if parts
        else [low_shape],
        cost_estimate=pl.CostEstimate(
            flops=10 * frames * width, bytes_accessed=14 * frames * width, transcendentals=0
        ),
        compiler_params=pltpu.CompilerParams(vmem_limit_bytes=32 * 2**20),
        name="norm_fwd",
    )(resid, gain[None], *parts)
    return result if parts else (resid, result[0])


def norm_backward_kernel(has_grad, parts, *refs):
    resid_ref, gain_ref = refs[0], refs[1]
    resid = resid_ref[...]
    upstream = add_terms([ref[...] for ref in refs[2 : 2 + parts]])
    out_ref, low_ref, gain_grad_ref = refs[-3:]
    centre = resid - jnp.mean(resid, -1, keepdims=True)
    inverse = lax.rsqrt(jnp.mean(centre * centre, -1, keepdims=True) + norm_eps)
    normed = centre * inverse
    scaled = upstream * gain_ref[...]
    step = inverse * (
        scaled
        - jnp.mean(scaled, -1, keepdims=True)
        - normed * jnp.mean(scaled * normed, -1, keepdims=True)
    )
    if has_grad:
        step = refs[2 + parts][...] + step
    out_ref[...] = step
    low_ref[...] = step.astype(jnp.bfloat16)
    rows, width = resid.shape
    term = jnp.sum((upstream * normed).reshape(rows // 8, 8, width), axis=0)

    @pl.when(pl.program_id(0) == 0)
    def _():
        gain_grad_ref[...] = term

    @pl.when(pl.program_id(0) > 0)
    def _():
        gain_grad_ref[...] = gain_grad_ref[...] + term


def norm_backward(resid, gain, upstream, resid_grad=None):
    frames, width = resid.shape
    rows = min(256, frames)
    block = pl.BlockSpec((rows, width), lambda i: (i, 0))
    extra = [] if resid_grad is None else [resid_grad]
    out_grad, low_grad, gain_grad = pl.pallas_call(
        functools.partial(norm_backward_kernel, bool(extra), len(upstream)),
        grid=(frames // rows,),
        in_specs=[block, pl.BlockSpec((1, width), lambda i: (0, 0))]
        + [block] * (len(upstream) + len(extra)),
        out_specs=[block, block, pl.BlockSpec((8, width), lambda i: (0, 0))],
        out_shape=[
            jax.ShapeDtypeStruct((frames, width), jnp.float32),
            jax.ShapeDtypeStruct((frames, width), jnp.bfloat16),
            jax.ShapeDtypeStruct((8, width), jnp.float32),
        ],
        cost_estimate=pl.CostEstimate(
            flops=20 * frames * width, bytes_accessed=18 * frames * width, transcendentals=0
        ),
        compiler_params=pltpu.CompilerParams(vmem_limit_bytes=40 * 2**20),
        name="norm_bwd",
    )(resid, gain[None], *upstream, *extra)
    return (out_grad, low_grad, jnp.sum(gain_grad, 0))


def dot_nt(left, right):
    return lax.dot_general(
        left, right, (((1,), (1,)), ((), ())), preferred_element_type=jnp.float32
    )


def dot_nn(left, right):
    return jnp.dot(left, right, preferred_element_type=jnp.float32)


def head_lanes(block, head):
    lane = lax.broadcasted_iota(jnp.int32, block.shape, 1)
    keep = lane >= HEAD_DIM if head else lane < HEAD_DIM
    return jnp.where(keep, block, jnp.zeros_like(block))


def attend_forward_kernel(masked, len_ref, q_ref, k_ref, v_ref, out_ref, log_ref):
    queries, keys_in = q_ref[...], k_ref[...]
    values_t = v_ref[...].T
    outputs = []
    for head in range(2):
        scores = dot_nt(keys_in, head_lanes(queries, head))
        if masked:
            place = lax.broadcasted_iota(jnp.int32, scores.shape, 0)
            scores = jnp.where(place < len_ref[0], scores, masked_score)
        largest = jnp.max(scores, 0, keepdims=True)
        exp_scores = jnp.exp2((scores - largest) * exp_scale)
        totals = jnp.sum(exp_scores, 0, keepdims=True)
        part = dot_nn(
            values_t[head * HEAD_DIM : (head + 1) * HEAD_DIM], exp_scores.astype(jnp.bfloat16)
        )
        outputs.append(part / totals)
        log_ref[0, head : head + 1, :] = largest * exp_scale + jnp.log2(totals)
    out_ref[...] = jnp.concatenate(outputs, 0).T.astype(jnp.bfloat16)


def attend_forward(lengths, queries, q_at, keys_in, k_at, values_in, v_at, width, masked):
    frames, keys = queries.shape[0], keys_in.shape[0]
    rows = min(256, frames)
    pairs = width // LANES
    q_at, k_at, v_at = q_at // LANES, k_at // LANES, v_at // LANES
    return pl.pallas_call(
        functools.partial(attend_forward_kernel, masked),
        grid=(pairs, frames // rows),
        in_specs=[
            pl.BlockSpec(memory_space=pltpu.SMEM),
            pl.BlockSpec((rows, LANES), lambda p, i: (i, q_at + p)),
            pl.BlockSpec((keys, LANES), lambda p, i: (0, k_at + p)),
            pl.BlockSpec((keys, LANES), lambda p, i: (0, v_at + p)),
        ],
        out_specs=[
            pl.BlockSpec((rows, LANES), lambda p, i: (i, p)),
            pl.BlockSpec((1, 8, rows), lambda p, i: (p, 0, i)),
        ],
        out_shape=[
            jax.ShapeDtypeStruct((frames, width), jnp.bfloat16),
            jax.ShapeDtypeStruct((pairs, 8, frames), jnp.float32),
        ],
        cost_estimate=pl.CostEstimate(
            flops=16 * width * frames * keys,
            bytes_accessed=8 * frames * width,
            transcendentals=frames * keys * width // HEAD_DIM,
        ),
        compiler_params=pltpu.CompilerParams(vmem_limit_bytes=40 * 2**20),
        name="attend_fwd",
    )(lengths, queries, keys_in, values_in)


def attend_backward_kernel(
    masked, split, len_ref, q_ref, k_ref, v_ref, o_ref, g_ref, log_ref, *refs
):
    if split:
        dq_ref, dkv_ref, dk_acc, dv_acc, keys_t = refs
    else:
        dkv_ref, dk_acc, dv_acc, keys_t = refs
    pair, step = pl.program_id(0), pl.program_id(1)
    queries, keys_in, values_in = q_ref[...], k_ref[...], v_ref[...]
    out_grad = g_ref[...]
    rows = queries.shape[0]

    @pl.when(step == 0)
    def _():
        keys_t[...] = keys_in.T

    product = (out_grad.astype(jnp.float32) * o_ref[...].astype(jnp.float32)).T
    probs, grads, q_heads, g_heads, dq_parts = [], [], [], [], []
    for head in range(2):
        q_head, g_head = head_lanes(queries, head), head_lanes(out_grad, head)
        span = slice(head * HEAD_DIM, (head + 1) * HEAD_DIM)
        scores = dot_nt(keys_in, q_head) * exp_scale - log_ref[0, head : head + 1, :]
        if masked:
            place = lax.broadcasted_iota(jnp.int32, scores.shape, 0)
            scores = jnp.where(place < len_ref[0], scores, masked_score)
        prob = jnp.exp2(scores)
        delta = jnp.sum(product[span], 0, keepdims=True)
        grad = (prob * (dot_nt(values_in, g_head) - delta)).astype(jnp.bfloat16)
        dq_parts.append(dot_nn(keys_t[span, :], grad))
        probs.append(prob.astype(jnp.bfloat16))
        grads.append(grad)
        q_heads.append(q_head)
        g_heads.append(g_head)
    dq = (jnp.concatenate(dq_parts, 0) * score_scale).T.astype(jnp.bfloat16)
    dk = dot_nn(jnp.concatenate(grads, 1), jnp.concatenate(q_heads, 0))
    dv = dot_nn(jnp.concatenate(probs, 1), jnp.concatenate(g_heads, 0))
    width = dkv_ref.shape[1] // (2 if split else 3)
    place = pl.multiple_of(pair * LANES, LANES)
    if split:
        dq_ref[...] = dq
        k_at, v_at = place, place + width
    else:
        dkv_ref[pl.ds(pl.multiple_of(step * rows, rows), rows), pl.ds(place, LANES)] = dq
        k_at, v_at = place + width, place + 2 * width

    @pl.when(step == 0)
    def _():
        dk_acc[...] = dk
        dv_acc[...] = dv

    @pl.when(step > 0)
    def _():
        dk_acc[...] = dk_acc[...] + dk
        dv_acc[...] = dv_acc[...] + dv

    @pl.when(step == pl.num_programs(1) - 1)
    def _():
        dkv_ref[:, pl.ds(pl.multiple_of(k_at, LANES), LANES)] = (
            dk_acc[...] * score_scale
        ).astype(jnp.bfloat16)
        dkv_ref[:, pl.ds(pl.multiple_of(v_at, LANES), LANES)] = dv_acc[...].astype(jnp.bfloat16)


def attend_backward(
    lengths, queries, q_at, keys_in, k_at, values_in, v_at, outputs, out_grad, logs, width, split
):
    frames, keys = queries.shape[0], keys_in.shape[0]
    rows = min(256, frames)
    pairs = width // LANES
    q_at, k_at, v_at = q_at // LANES, k_at // LANES, v_at // LANES
    row_block = pl.BlockSpec((rows, LANES), lambda p, i: (i, p))
    outs = [jax.ShapeDtypeStruct((keys, width * (2 if split else 3)), jnp.bfloat16)]
    out_specs = [pl.BlockSpec(outs[0].shape, lambda p, i: (0, 0))]
    if split:
        outs = [jax.ShapeDtypeStruct((frames, width), jnp.bfloat16)] + outs
        out_specs = [row_block] + out_specs
    return pl.pallas_call(
        functools.partial(attend_backward_kernel, split, split),
        grid=(pairs, frames // rows),
        in_specs=[
            pl.BlockSpec(memory_space=pltpu.SMEM),
            pl.BlockSpec((rows, LANES), lambda p, i: (i, q_at + p)),
            pl.BlockSpec((keys, LANES), lambda p, i: (0, k_at + p)),
            pl.BlockSpec((keys, LANES), lambda p, i: (0, v_at + p)),
            row_block,
            row_block,
            pl.BlockSpec((1, 8, rows), lambda p, i: (p, 0, i)),
        ],
        out_specs=out_specs,
        out_shape=outs,
        scratch_shapes=[
            pltpu.VMEM((keys, LANES), jnp.float32),
            pltpu.VMEM((keys, LANES), jnp.float32),
            pltpu.VMEM((LANES, keys), jnp.bfloat16),
        ],
        cost_estimate=pl.CostEstimate(
            flops=40 * width * frames * keys,
            bytes_accessed=16 * frames * width,
            transcendentals=frames * keys * width // HEAD_DIM,
        ),
        compiler_params=pltpu.CompilerParams(vmem_limit_bytes=48 * 2**20),
        name="attend_bwd",
    )(lengths, queries, keys_in, values_in, outputs, out_grad, logs)


def frame_embedding(layout, frames, width, feature, step):
    half = width // 2
    frequency = jnp.exp(-math.log(10000.0) * (feature % half).astype(jnp.float32) / half)
    is_sin = feature < half

    def embed(position):
        angles = position[:, None] * frequency[None]
        return jnp.where(is_sin[None], jnp.sin(angles), jnp.cos(angles))

    return embed(jnp.arange(frames, dtype=jnp.float32)) + embed(step.astype(jnp.float32)[None])


def gelu_parts(hidden):
    scale = math.sqrt(2.0 / math.pi)
    square = hidden * hidden
    bend = jnp.tanh(scale * (hidden + 0.044715 * (square * hidden)))
    half_up = 0.5 * (1.0 + bend)
    slope = half_up + 0.5 * hidden * (1.0 - bend * bend) * scale * (1.0 + 3.0 * 0.044715 * square)
    return (as_low(hidden * half_up), as_low(slope))


def dot_tn(left, right):
    return lax.dot_general(
        left, right, (((0,), (0,)), ((), ())), preferred_element_type=jnp.float32
    )


def adam_update(master, first_moment, second_moment, average, gradient, factor, step_rate):
    clipped = gradient * factor
    first_new = beta_first * first_moment + (1.0 - beta_first) * clipped
    second_new = beta_second * second_moment + (1.0 - beta_second) * clipped * clipped
    first_hat = first_new / (1.0 - beta_first**STEP)
    second_hat = second_new / (1.0 - beta_second**STEP)
    master_new = master - step_rate * (
        first_hat / (jnp.sqrt(second_hat) + adam_eps) + weight_decay * master
    )
    return (
        master_new,
        first_new,
        second_new,
        average_keep * average + (1.0 - average_keep) * master_new,
    )


def local(
    latents,
    noise_draw,
    timesteps,
    text_ids,
    text_len,
    item_counts,
    text_table,
    io_weight,
    io_first,
    io_second,
    io_average,
    norm_gains,
    gains_first,
    gains_second,
    gains_average,
    col_weight,
    col_first,
    col_second,
    col_average,
    text_weight,
    text_first,
    text_second,
    text_average,
    row_weight,
    row_first,
    row_second,
    row_average,
):
    items, channels, frame_part = latents.shape
    layout = Layout(items)
    frames = frame_part * layout.mp_size
    levels, block = col_weight.shape[0], col_weight.shape[1]
    part = col_weight.shape[3]
    model_width = block * layout.dp_size
    gain_count = norm_gains.shape[0]
    text_block = text_weight.shape[1]
    item = layout.item

    col_low, row_low, text_low = as_low(col_weight), as_low(row_weight), as_low(text_weight)
    small = jnp.concatenate(
        [
            as_low(io_weight).reshape(2 * channels, block),
            as_low(norm_gains),
            jnp.full((1, block), item_counts[0], jnp.bfloat16),
        ],
        0,
    )
    small = gather_dp(layout, small[None], 0, layout.masks)
    small = jnp.swapaxes(small, 0, 1).reshape(2 * channels + gain_count + 1, model_width)
    io_w = [small[:channels], small[channels : 2 * channels]]
    gain_w = small[2 * channels : 2 * channels + gain_count].astype(jnp.float32)
    item_total = jnp.sum(small[-1].astype(jnp.float32)) / block

    qkv_w, mid_w, up_w, down_w = [], [], [], []
    text_w = None
    for level in range(levels):
        qkv_w.append(
            gather_last_item(layout, col_low[level, :, 0:3].reshape(block, 3 * part), 0)
        )
        mid_w.append(
            gather_last_dp(
                layout,
                jnp.stack([row_low[level, 0], col_low[level, :, 3], row_low[level, 1]]),
                1,
            )
        )
        if level == 0:
            text_w = gather_last_dp(
                layout, jnp.swapaxes(text_low, 0, 1).reshape(text_block, 2 * levels * part), 0
            )
        up_w.append(gather_last_item(layout, col_low[level, :, 4:].reshape(block, -1), 0))
        down_w.append(
            gather_last_dp(
                layout, jnp.swapaxes(row_low[level, 2:], 0, 1).reshape(block, -1), 0
            )
        )

    table_rows = text_table.shape[0]
    local_ids = text_ids - lax.axis_index("mp") * table_rows
    inside = (local_ids >= 0) & (local_ids < table_rows)
    picked = text_table[jnp.clip(local_ids, 0, table_rows - 1)]
    picked = jnp.where(inside[..., None], picked, jnp.zeros_like(picked))
    text_feat = lax.dynamic_index_in_dim(lax.psum(picked, "mp"), item, 0, keepdims=False)
    tokens = text_feat.shape[0]
    text_feat = jnp.take(
        text_feat.reshape(tokens, layout.dp_size, text_block), layout.blocks(), axis=1
    ).reshape(tokens, layout.dp_size * text_block)
    length = lax.dynamic_slice_in_dim(text_len, item, 1)

    steps = timesteps[item]
    alpha_bar = jnp.sum(jnp.where(steps == jnp.arange(1000), plan(), 0.0))
    alpha_all = jnp.sum(
        jnp.where(timesteps[:, None] == jnp.arange(1000)[None, :], plan()[None, :], 0.0), -1
    )
    noisy = as_low(
        jnp.sqrt(alpha_all)[:, None, None] * latents
        + jnp.sqrt(1.0 - alpha_all)[:, None, None] * noise_draw
    )
    noisy = lax.dynamic_index_in_dim(
        lax.all_gather(noisy, "mp", axis=2, tiled=True), item, 0, keepdims=False
    )
    noise = lax.dynamic_index_in_dim(
        lax.all_gather(noise_draw, "mp", axis=2, tiled=True), item, 0, keepdims=False
    )
    feature = (layout.blocks()[:, None] * block + jnp.arange(block)[None]).reshape(model_width)
    resid = dot_tn(noisy, io_w[0]) + frame_embedding(layout, frames, model_width, feature, steps)

    text_kv = [as_low(dot_nn(text_feat, weight)) for weight in text_w]

    kept_all = []
    parts = ()
    for level in range(levels):
        resid_self, normed_self = norm_forward(resid, gain_w[3 * level], parts)
        qkv = [as_low(dot_nn(normed_self, weight)) for weight in qkv_w[level]]
        attended, self_log = [], []
        for whole in qkv:
            out, log = attend_forward(
                length, whole, 0, whole, part, whole, 2 * part, part, False
            )
            attended.append(out)
            self_log.append(log)
        total = add_terms([dot_nt(o, w[0]) for o, w in zip(attended, mid_w[level])])
        parts = layout.rank_pair(as_low(total))
        resid_cross, normed_cross = norm_forward(resid_self, gain_w[3 * level + 1], parts)
        cross_query = [as_low(dot_nn(normed_cross, w[1])) for w in mid_w[level]]
        key_at = 2 * level * part
        cross_out, cross_log = [], []
        for query, text in zip(cross_query, text_kv):
            out, log = attend_forward(
                length, query, 0, text, key_at, text, key_at + part, part, True
            )
            cross_out.append(out)
            cross_log.append(log)
        total = add_terms([dot_nt(o, w[2]) for o, w in zip(cross_out, mid_w[level])])
        parts = layout.rank_pair(as_low(total))
        resid_mlp, normed_mlp = norm_forward(resid_cross, gain_w[3 * level + 2], parts)
        active, slope = [], []
        for weight in up_w[level]:
            low_value, low_slope = gelu_parts(dot_nn(normed_mlp, weight))
            active.append(low_value)
            slope.append(low_slope)
        total = add_terms([dot_nt(a, w) for a, w in zip(active, down_w[level])])
        parts = layout.rank_pair(as_low(total))
        resid = resid_mlp
        kept_all.append(
            (
                (resid_self, normed_self, qkv, attended, self_log),
                (resid_cross, normed_cross, cross_query, cross_out, cross_log),
                (resid_mlp, normed_mlp, active, slope),
            )
        )
    resid, final_low = norm_forward(resid, gain_w[3 * levels], parts)
    predicted = dot_nt(io_w[1], final_low)
    residual_error = predicted - noise
    snr_ratio = alpha_bar / (1.0 - alpha_bar)
    loss_weight = jnp.minimum(snr_ratio, snr_limit) / snr_ratio
    valid = (item < item_counts[0]).astype(jnp.float32)
    item_scale = valid * loss_weight / (channels * frames)
    loss_part = item_scale * jnp.sum(residual_error * residual_error)
    pred_grad = as_low((2.0 * item_scale / item_total) * residual_error)
    out_proj_grad = dot_nn(pred_grad, final_low)
    final_grad = dot_tn(pred_grad, io_w[1])

    gain_grads = [None] * gain_count
    resid_grad, branch_grad, gain_grads[3 * levels] = norm_backward(
        resid, gain_w[3 * levels], [final_grad]
    )
    qkv_g, mid_g, up_g, down_g = ([None] * levels for _ in range(4))
    text_grads = [[None] * levels for _ in range(items)]
    for level in reversed(range(levels)):
        kept_self, kept_cross, kept_mlp = kept_all[level]
        resid_mlp, normed_mlp, active, slope = kept_mlp
        down_g[level] = scatter_first_item(
            layout, [as_low(dot_tn(branch_grad, a)) for a in active]
        )
        hidden_grad = [
            as_low(dot_nn(branch_grad, w) * s.astype(jnp.float32))
            for w, s in zip(down_w[level], slope)
        ]
        total = add_terms([dot_nt(z, w) for z, w in zip(hidden_grad, up_w[level])])
        upstream = layout.rank_pair(as_low(total))
        up_g[level] = scatter_first_dp(
            layout, [as_low(dot_tn(normed_mlp, z)) for z in hidden_grad]
        )
        resid_grad, branch_grad, gain_grads[3 * level + 2] = norm_backward(
            resid_mlp, gain_w[3 * level + 2], upstream, resid_grad
        )

        resid_cross, normed_cross, cross_query, cross_out, cross_log = kept_cross
        key_at = 2 * level * part
        cross_w_grad, query_w_grad, query_grads = [], [], []
        for index in range(items):
            weight = mid_w[level][index]
            cross_w_grad.append(dot_tn(branch_grad, cross_out[index]))
            out_grad = as_low(dot_nn(branch_grad, weight[2]))
            text = text_kv[index]
            query_grad, text_grads[index][level] = attend_backward(
                length,
                cross_query[index],
                0,
                text,
                key_at,
                text,
                key_at + part,
                cross_out[index],
                out_grad,
                cross_log[index],
                part,
                True,
            )
            query_grads.append(query_grad)
            query_w_grad.append(dot_tn(normed_cross, query_grad))
        total = add_terms([dot_nt(q, w[1]) for q, w in zip(query_grads, mid_w[level])])
        upstream = layout.rank_pair(as_low(total))
        resid_grad, branch_grad, gain_grads[3 * level + 1] = norm_backward(
            resid_cross, gain_w[3 * level + 1], upstream, resid_grad
        )

        resid_self, normed_self, qkv, attended, self_log = kept_self
        self_w_grad, qkv_grads = [], []
        for index in range(items):
            weight, whole = mid_w[level][index], qkv[index]
            self_w_grad.append(dot_tn(branch_grad, attended[index]))
            out_grad = as_low(dot_nn(branch_grad, weight[0]))
            (grads,) = attend_backward(
                length,
                whole,
                0,
                whole,
                part,
                whole,
                2 * part,
                attended[index],
                out_grad,
                self_log[index],
                part,
                False,
            )
            qkv_grads.append(grads)
        mid_g[level] = scatter_first_item(
            layout,
            [
                as_low(jnp.concatenate(three, 1))
                for three in zip(self_w_grad, query_w_grad, cross_w_grad)
            ],
        )
        total = add_terms([dot_nt(z, w) for z, w in zip(qkv_grads, qkv_w[level])])
        upstream = layout.rank_pair(as_low(total))
        qkv_g[level] = scatter_first_dp(
            layout, [as_low(dot_tn(normed_self, z)) for z in qkv_grads]
        )
        resid_grad, branch_grad, gain_grads[3 * level] = norm_backward(
            resid_self, gain_w[3 * level], upstream, resid_grad
        )

    text_g = scatter_first_item(
        layout,
        [as_low(dot_tn(text_feat, jnp.concatenate(grads, 1))) for grads in text_grads],
    )
    in_proj_grad = dot_nn(noisy, branch_grad)
    small_grad = jnp.concatenate([in_proj_grad, out_proj_grad, jnp.stack(gain_grads)], 0)
    small_grad = small_grad.reshape(-1, layout.dp_size, block).swapaxes(0, 1)
    small_grad = scatter_first_item(layout, [small_grad, small_grad])[0]

    io_grad = small_grad[: 2 * channels].reshape(2, channels, block)
    gain_grad = small_grad[2 * channels :]
    col_grad = jnp.stack(
        [
            jnp.concatenate(
                [
                    qkv_g[level].reshape(block, 3, part),
                    mid_g[level][:, None, part : 2 * part],
                    up_g[level].reshape(block, -1, part),
                ],
                1,
            )
            for level in range(levels)
        ]
    )
    kv_grad = jnp.swapaxes(text_g.reshape(text_block, levels, 2, part), 0, 1)
    row_grad = jnp.stack(
        [
            jnp.concatenate(
                [
                    mid_g[level][None, :, :part],
                    mid_g[level][None, :, 2 * part :],
                    jnp.swapaxes(down_g[level].reshape(block, -1, part), 0, 1),
                ],
                0,
            )
            for level in range(levels)
        ]
    )

    first_owner = (lax.axis_index("mp") == 0).astype(jnp.float32)
    square = add_terms(
        [
            jnp.sum(grad * grad)
            for group in (qkv_g, mid_g, up_g, down_g, [text_g])
            for grad in group
        ]
    )
    square = square + first_owner * jnp.sum(small_grad * small_grad)
    loss_part = loss_part * (layout.rank == 0).astype(jnp.float32)
    totals = lax.psum(jnp.stack([square, loss_part]), ("dp", "mp"))
    grad_norm = jnp.sqrt(totals[0])
    factor = jnp.minimum(1.0, clip_limit / (grad_norm + 1e-06))
    results = [totals[1], item_total, grad_norm]
    io_updated = adam_update(
        io_weight, io_first, io_second, io_average, io_grad, factor, matrix_rate
    )
    results.extend(
        [io_updated[0], io_updated[1], io_updated[2][0], io_updated[2][1], io_updated[3]]
    )
    results.extend(
        adam_update(
            norm_gains, gains_first, gains_second, gains_average, gain_grad, factor, gain_rate
        )
    )
    results.extend(
        adam_update(col_weight, col_first, col_second, col_average, col_grad, factor, matrix_rate)
    )
    results.extend(
        adam_update(
            text_weight, text_first, text_second, text_average, kv_grad, factor, matrix_rate
        )
    )
    results.extend(
        adam_update(row_weight, row_first, row_second, row_average, row_grad, factor, row_rate)
    )
    return tuple(results)


def solution(mesh):
    return jax.shard_map(
        local,
        mesh=mesh,
        in_specs=(
            P("dp", None, "mp"),
            P("dp", None, "mp"),
            P("dp"),
            P("dp", None),
            P("dp"),
            P("dp"),
            P("mp", None),
            P(None, None, "dp"),
            P(None, None, "dp"),
            P(None, None, "dp"),
            P(None, None, "dp"),
            P(None, "dp"),
            P(None, "dp"),
            P(None, "dp"),
            P(None, "dp"),
            P(None, "dp", None, "mp"),
            P(None, "dp", None, "mp"),
            P(None, "dp", None, "mp"),
            P(None, "dp", None, "mp"),
            P(None, "dp", None, "mp"),
            P(None, "dp", None, "mp"),
            P(None, "dp", None, "mp"),
            P(None, "dp", None, "mp"),
            P(None, None, "dp", "mp"),
            P(None, None, "dp", "mp"),
            P(None, None, "dp", "mp"),
            P(None, None, "dp", "mp"),
        ),
        out_specs=(
            P(),
            P(),
            P(),
            P(None, None, "dp"),
            P(None, None, "dp"),
            P(None, "dp"),
            P(None, "dp"),
            P(None, None, "dp"),
            P(None, "dp"),
            P(None, "dp"),
            P(None, "dp"),
            P(None, "dp"),
            P(None, "dp", None, "mp"),
            P(None, "dp", None, "mp"),
            P(None, "dp", None, "mp"),
            P(None, "dp", None, "mp"),
            P(None, "dp", None, "mp"),
            P(None, "dp", None, "mp"),
            P(None, "dp", None, "mp"),
            P(None, "dp", None, "mp"),
            P(None, None, "dp", "mp"),
            P(None, None, "dp", "mp"),
            P(None, None, "dp", "mp"),
            P(None, None, "dp", "mp"),
        ),
        check_vma=False,
    )
```

time: 2350 us -> 1200 us (0.51)
  waiting for transfers between devices: 1470 us -> 385 us
  Pallas kernels: 0 us -> 237 us
  matrix products: 372 us -> 195 us
  local copies, waits for them, and re-layouts: 188 us -> 75.7 us
  starting transfers between devices: 3.91 us -> 98.2 us
  blocking collectives: 117 us -> 48.8 us
  other arithmetic: 171 us -> 118 us
    reduce_scatter x15 -> x0, waiting for transfers between devices: 748 us -> none  [the longest x6 255 us: sum_rows(): lax.psum_scatter(tensor.astype(jnp.bfloat16), 'mp', scatter_dimension=1,...]
    all_gather x15 -> x0, waiting for transfers between devices: 565 us -> none  [the longest x6 207 us: gather_grads(): return lax.all_gather(as_low(tensor), 'mp', axis=1, tiled=True)]
    ppermute x0 -> x100, waiting for transfers between devices: none -> 385 us  [exchange(): return lax.ppermute(tensor, axis, [(i, i ^ mask) for i in range(size)])]
    pallas_call x0 -> x30, Pallas kernels: none -> 237 us  [the longest x8 93.1 us: attend_backward(): pl.pallas_call(functools.partial(attend_backward_kernel, split, split), g...]
    dot_general x101 -> x81, matrix products: 372 us -> 195 us  [the longest x28 93.4 us: dot_tn(): lax.dot_general(left, right, (((0,), (0,)), ((), ())), preferred_element_...]
    unnamed x35 -> x1, waiting for transfers between devices: 126 us -> 0.02 us
    ppermute x0 -> x100, starting transfers between devices: none -> 98.1 us  [exchange(): return lax.ppermute(tensor, axis, [(i, i ^ mask) for i in range(size)])]
    convert_element_type x24 -> x2, other arithmetic: 71.3 us -> 1.43 us  [as_low(): return tensor.astype(jnp.bfloat16)]
  transfers between devices with their start and end apart: 33 -> 101, of which waited for: 32 -> 45; matrix products, arithmetic and copies ran while one was open for 7% -> 26% of each run, Pallas kernels for 0% -> 17%
where the time goes in v1:
time: 1200 us; the launch traced here: 1190 us
  waiting for transfers between devices  385 us (32%)
  Pallas kernels  237 us (20%)
  matrix products  195 us (16%)
  other arithmetic  118 us (10%)
  starting transfers between devices  98.2 us (8%)
  local copies, waits for them, and re-layouts  75.7 us (6%)
  blocking collectives  48.8 us (4%)
  between operations  32.3 us (3%)
    ppermute x100, waiting for transfers between devices, exchange(): return lax.ppermute(tensor, axis, [(i, i ^ mask) for i in range(size)])  385 us
    ppermute x100, starting transfers between devices, exchange(): return lax.ppermute(tensor, axis, [(i, i ^ mask) for i in range(size)])  98.1 us
    dot_general x28, matrix products, dot_tn(): lax.dot_general(left, right, (((0,), (0,)), ((), ())), preferred_element_...  93.4 us
    pallas_call x8, Pallas kernels, attend_backward(): pl.pallas_call(functools.partial(attend_backward_kernel, split, split), g...  93.1 us
    pallas_call x8, Pallas kernels, attend_forward(): pl.pallas_call(functools.partial(attend_forward_kernel, masked), grid=(pa...  82.6 us
    dot_general x28, matrix products, dot_nn(): return jnp.dot(left, right, preferred_element_type=jnp.float32)  60.8 us
    pallas_call x7, Pallas kernels, norm_backward(): pl.pallas_call(functools.partial(norm_backward_kernel, bool(extra), len(u...  44.7 us
    convert_element_type x23, other arithmetic, halve(): send = add_terms([term[half:] for term in terms]).astype(kind)  40.9 us
  transfers between devices with their start and end apart: 101, of which 45 were waited for; matrix products, arithmetic and copies ran while one was open for 26% of the time, Pallas kernels for 17%

profile of v1, /device:TPU:0, one launch (start us, length us, event | category | flops | bytes accessed | tf_op | source)
XLA Modules:
  0.0 1189.6 jit_solution(868449921932312688)
XLA Ops:
  81.8 30.2 %add_add_fusion.refs_0_ = f32[1024,1024]{1,0:T(8,128)S(1)} fusion(bf16[20,1024]{1,0:T(8,128)(2,1)S(1)} %bitcast.375, f32[1024]{0:T(1024)S(1)} %get-tuple-element.273, f32[1024]{0:T(1024)S(1)} %get-tuple-element.274, pred[1024]{0:T(1024)(128)(4,1)S(1)} %bitcast_compare_fusion, bf16[2,20,1024]{2,1,0:T(8,128)(2,1)S(1)} %all_gather.6, s32[]{:T(128)S(6)} %select_n.74), kind=kOutput, calls=%fused_computation.66 | convolution fusion | flops 46137344 | bytes 4301828 | tf_op jit(solution)/shard_map/dot_general | solution.py:411
  121.5 14.2 %attend_fwd.8 = (bf16[1024,256]{1,0:T(8,128)(2,1)S(1)}, f32[2,8,1024]{2,1,0:T(8,128)S(1)}) custom-call(s32[1]{0:T(128)} %dynamic_slice.20.len_ref, bf16[1024,768]{1,0:T(8,128)(2,1)S(1)} %convolution_convert_fusion.17.q_ref.k_ref.v_ref, bf16[1024,768]{1,0:T(8,128)(2,1)S(1)} %convolution_convert_fusion.17.q_ref.k_ref.v_ref, ...), custom_call_target="tpu_custom_call" | custom-call | flops 4294967296 | bytes 2097152 | tf_op jit(solution)/shard_map/attend_fwd/pallas_call | solution.py:257
  136.7 15.8 %collective-permute-done.9 = bf16[1024,768]{0,1:T(8,128)(2,1)S(1)} collective-permute-done((bf16[1024,768]{0,1:T(8,128)(2,1)S(1)}, bf16[1024,768]{0,1:T(8,128)(2,1)S(1)}, u32[]{:S(2)}, u32[]{:S(2)}) %collective-permute-start.9) | collective-permute-done | bytes 1572896 | tf_op jit(solution)/shard_map/ppermute | solution.py:44
  154.3 14.2 %attend_fwd.9 = (bf16[1024,256]{1,0:T(8,128)(2,1)S(1)}, f32[2,8,1024]{2,1,0:T(8,128)S(1)}) custom-call(s32[1]{0:T(128)} %dynamic_slice.20.len_ref, bf16[1024,768]{1,0:T(8,128)(2,1)S(1)} %convolution_convert_fusion.16.q_ref.k_ref.v_ref, bf16[1024,768]{1,0:T(8,128)(2,1)S(1)} %convolution_convert_fusion.16.q_ref.k_ref.v_ref, ...), custom_call_target="tpu_custom_call" | custom-call | flops 4294967296 | bytes 2097152 | tf_op jit(solution)/shard_map/attend_fwd/pallas_call | solution.py:257
  177.9 10.7 collective-permute-done.22
  243.8 11.0 collective-permute-done.29
  291.3 20.7 %collective-permute-done.24 = bf16[512,1024]{0,1:T(8,128)(2,1)S(1)} collective-permute-done((bf16[512,1024]{0,1:T(8,128)(2,1)S(1)}, bf16[512,1024]{0,1:T(8,128)(2,1)S(1)}, u32[]{:S(2)}, u32[]{:S(2)}) %collective-permute-start.24) | collective-permute-done | bytes 1048608 | tf_op jit(solution)/shard_map/ppermute | solution.py:44
  322.3 17.0 %collective-permute-done.36 = bf16[3,512,256]{1,2,0:T(8,128)(2,1)S(1)} collective-permute-done((bf16[3,512,256]{1,2,0:T(8,128)(2,1)S(1)}, bf16[3,512,256]{1,2,0:T(8,128)(2,1)S(1)}, u32[]{:S(2)}, u32[]{:S(2)}) %collective-permute-start.36) | collective-permute-done | bytes 786464 | tf_op jit(solution)/shard_map/ppermute | solution.py:44
  340.9 17.2 %collective-permute-done.37 = bf16[3,512,256]{1,2,0:T(8,128)(2,1)S(1)} collective-permute-done((bf16[3,512,256]{1,2,0:T(8,128)(2,1)S(1)}, bf16[3,512,256]{1,2,0:T(8,128)(2,1)S(1)}, u32[]{:S(2)}, u32[]{:S(2)}) %collective-permute-start.37) | collective-permute-done | bytes 786464 | tf_op jit(solution)/shard_map/ppermute | solution.py:44
  360.0 12.6 %collective-permute-done.35 = bf16[1024,768]{0,1:T(8,128)(2,1)S(1)} collective-permute-done((bf16[1024,768]{0,1:T(8,128)(2,1)S(1)}, bf16[1024,768]{0,1:T(8,128)(2,1)S(1)}, u32[]{:S(2)}, u32[]{:S(2)}) %collective-permute-start.35) | collective-permute-done | bytes 1572896 | tf_op jit(solution)/shard_map/ppermute | solution.py:44
  374.5 14.4 %attend_fwd.13 = (bf16[1024,256]{1,0:T(8,128)(2,1)S(1)}, f32[2,8,1024]{2,1,0:T(8,128)S(1)}) custom-call(s32[1]{0:T(128)} %dynamic_slice.20.len_ref, bf16[1024,768]{1,0:T(8,128)(2,1)S(1)} %convolution_convert_fusion.14.q_ref.k_ref.v_ref, bf16[1024,768]{1,0:T(8,128)(2,1)S(1)} %convolution_convert_fusion.14.q_ref.k_ref.v_ref, ...), custom_call_target="tpu_custom_call" | custom-call | flops 4294967296 | bytes 2097152 | tf_op jit(solution)/shard_map/attend_fwd/pallas_call | solution.py:257
  390.8 14.2 %attend_fwd.12 = (bf16[1024,256]{1,0:T(8,128)(2,1)S(1)}, f32[2,8,1024]{2,1,0:T(8,128)S(1)}) custom-call(s32[1]{0:T(128)} %dynamic_slice.20.len_ref, bf16[1024,768]{1,0:T(8,128)(2,1)S(1)} %convolution_convert_fusion.15.q_ref.k_ref.v_ref, bf16[1024,768]{1,0:T(8,128)(2,1)S(1)} %convolution_convert_fusion.15.q_ref.k_ref.v_ref, ...), custom_call_target="tpu_custom_call" | custom-call | flops 4294967296 | bytes 2097152 | tf_op jit(solution)/shard_map/attend_fwd/pallas_call | solution.py:257
  409.7 17.6 %collective-permute-done.40 = bf16[128,1024]{0,1:T(8,128)(2,1)S(1)} collective-permute-done((bf16[128,1024]{0,1:T(8,128)(2,1)S(1)}, bf16[128,1024]{0,1:T(8,128)(2,1)S(1)}, u32[]{:S(2)}, u32[]{:S(2)}) %collective-permute-start.40) | collective-permute-done | bytes 262176 | tf_op jit(solution)/shard_map/ppermute | solution.py:44
  433.1 11.1 collective-permute-done.41
  483.7 23.9 %collective-permute-done.48 = bf16[512,1024]{0,1:T(8,128)(2,1)S(1)} collective-permute-done((bf16[512,1024]{0,1:T(8,128)(2,1)S(1)}, bf16[512,1024]{0,1:T(8,128)(2,1)S(1)}, u32[]{:S(2)}, u32[]{:S(2)}) %collective-permute-start.48) | collective-permute-done | bytes 1048608 | tf_op jit(solution)/shard_map/ppermute | solution.py:44
  512.2 13.4 %collective-permute-done.46 = bf16[1024,1024]{0,1:T(8,128)(2,1)S(1)} collective-permute-done((bf16[1024,1024]{0,1:T(8,128)(2,1)S(1)}, bf16[1024,1024]{0,1:T(8,128)(2,1)S(1)}, u32[]{:S(2)}, u32[]{:S(2)}) %collective-permute-start.46) | collective-permute-done | bytes 2097184 | tf_op jit(solution)/shard_map/ppermute | solution.py:44
  614.5 21.2 %collective-permute-done.87 = bf16[1024,1024]{0,1:T(8,128)(2,1)} collective-permute-done((bf16[1024,1024]{0,1:T(8,128)(2,1)}, bf16[1024,1024]{0,1:T(8,128)(2,1)}, u32[]{:S(2)}, u32[]{:S(2)}) %collective-permute-start.87) | collective-permute-done | bytes 2097184 | tf_op jit(solution)/shard_map/ppermute | solution.py:44
  667.5 10.3 collective-permute-done.81
  679.9 14.0 %collective-permute-done.89 = bf16[256,1024]{0,1:T(8,128)(2,1)S(1)} collective-permute-done((bf16[256,1024]{0,1:T(8,128)(2,1)S(1)}, bf16[256,1024]{0,1:T(8,128)(2,1)S(1)}, u32[]{:S(2)}, u32[]{:S(2)}) %collective-permute-start.89) | collective-permute-done | bytes 524320 | tf_op jit(solution)/shard_map/ppermute | solution.py:44
  708.2 16.3 %attend_bwd.11 = bf16[1024,768]{1,0:T(8,128)(2,1)S(1)} custom-call(s32[1]{0:T(128)} %dynamic_slice.20.len_ref, bf16[1024,768]{1,0:T(8,128)(2,1)S(1)} %copy-done.86, bf16[1024,768]{1,0:T(8,128)(2,1)S(1)} %copy-done.86, bf16[1024,768]{1,0:T(8,128)(2,1)S(1)} %copy-done.86, bf16[1024,256]{1,0:T(8,128)(2,1)S(1)} %copy-done.29, ...), custom_call_target="tpu_custom_call" | custom-call | flops 10737418240 | bytes 4194304 | tf_op jit(solution)/shard_map/attend_bwd/pallas_call | solution.py:360
  729.4 16.4 %attend_bwd.10 = bf16[1024,768]{1,0:T(8,128)(2,1)S(1)} custom-call(s32[1]{0:T(128)} %dynamic_slice.20.len_ref, bf16[1024,768]{1,0:T(8,128)(2,1)S(1)} %copy-done.82, bf16[1024,768]{1,0:T(8,128)(2,1)S(1)} %copy-done.82, bf16[1024,768]{1,0:T(8,128)(2,1)S(1)} %copy-done.82, bf16[1024,256]{1,0:T(8,128)(2,1)S(1)} %copy-done.23, ...), custom_call_target="tpu_custom_call" | custom-call | flops 10737418240 | bytes 4194304 | tf_op jit(solution)/shard_map/attend_bwd/pallas_call | solution.py:360
  981.9 16.3 %attend_bwd.15 = bf16[1024,768]{1,0:T(8,128)(2,1)S(1)} custom-call(s32[1]{0:T(128)} %dynamic_slice.20.len_ref, bf16[1024,768]{1,0:T(8,128)(2,1)S(1)} %copy-done.84, bf16[1024,768]{1,0:T(8,128)(2,1)S(1)} %copy-done.84, bf16[1024,768]{1,0:T(8,128)(2,1)S(1)} %copy-done.84, bf16[1024,256]{1,0:T(8,128)(2,1)S(1)} %copy-done.25, ...), custom_call_target="tpu_custom_call" | custom-call | flops 10737418240 | bytes 4194304 | tf_op jit(solution)/shard_map/attend_bwd/pallas_call | solution.py:360
  1003.9 16.7 %attend_bwd.14 = bf16[1024,768]{1,0:T(8,128)(2,1)S(1)} custom-call(s32[1]{0:T(128)} %dynamic_slice.20.len_ref, bf16[1024,768]{1,0:T(8,128)(2,1)S(1)} %copy-done.80, bf16[1024,768]{1,0:T(8,128)(2,1)S(1)} %copy-done.80, bf16[1024,768]{1,0:T(8,128)(2,1)S(1)} %copy-done.80, bf16[1024,256]{1,0:T(8,128)(2,1)S(1)} %copy-done.19, ...), custom_call_target="tpu_custom_call" | custom-call | flops 10737418240 | bytes 4194304 | tf_op jit(solution)/shard_map/attend_bwd/pallas_call | solution.py:360
  1116.6 37.3 %psum.15 = f32[2]{0:T(128)S(1)} all-reduce(f32[2]{0:T(128)S(1)} %pad_maximum_fusion.37), channel_id=1, replica_groups=mesh['dp'=8,'mp'=4] {'dp','mp'}, use_global_device_ids=true, to_apply=%region_24.26 | all-reduce | flops 2 | bytes 16 | tf_op jit(solution)/shard_map/psum | solution.py:738
  (989 shorter events, 750.8 us)
Async XLA Ops:
  7.2 186.3 %all-reduce.3.cloned.1.call-start = ((), (), s32[]{:S(2)}) async-start(), calls=%async_computation | async-start | bytes 786432 | tf_op jit(solution)/shard_map/psum | solution.py:516
  15.6 98.4 %collective-permute-start.13 = (bf16[96,1024]{1,0:T(8,128)(2,1)}, bf16[96,1024]{1,0:T(8,128)(2,1)}, u32[]{:S(2)}, u32[]{:S(2)}) collective-permute-start(bf16[96,1024]{1,0:T(8,128)(2,1)} %reshape.222), channel_id=1, source_target_pairs={{0,16},{4,20},{8,24},{12,28},{16,0},{20,4},{24,8},{28,12},{1,17},{... | collective-permute-start | bytes 589832 | tf_op jit(solution)/shard_map/ppermute | solution.py:44
  35.0 141.1 %collective-permute-start.19 = (bf16[128,1024]{0,1:T(8,128)(2,1)S(1)}, bf16[128,1024]{0,1:T(8,128)(2,1)S(1)}, u32[]{:S(2)}, u32[]{:S(2)}) collective-permute-start(bf16[128,1024]{0,1:T(8,128)(2,1)S(1)} %bitcast.320), channel_id=1, source_target_pairs={{0,16},{4,20},{8,24},{12,28},{16,0},{20,4},{24,8},{28,12},{1,17},{... | collective-permute-start | bytes 786440 | tf_op jit(solution)/shard_map/ppermute | solution.py:44
  115.5 55.5 %collective-permute-start.14 = (bf16[192,1024]{1,0:T(8,128)(2,1)S(1)}, bf16[192,1024]{1,0:T(8,128)(2,1)S(1)}, u32[]{:S(2)}, u32[]{:S(2)}) collective-permute-start(bf16[192,1024]{1,0:T(8,128)(2,1)S(1)} %pad_maximum_fusion.26), channel_id=1, source_target_pairs={{0,8},{4,12},{8,0},{12,4},{16,24},{20,28},{24,16},{28,20},{1,9},{5... | collective-permute-start | bytes 1179656 | tf_op jit(solution)/shard_map/ppermute | solution.py:44
  266.9 51.9 %collective-permute-start.33 = (bf16[3,256,256]{1,2,0:T(8,128)(2,1)S(1)}, bf16[3,256,256]{1,2,0:T(8,128)(2,1)S(1)}, u32[]{:S(2)}, u32[]{:S(2)}) collective-permute-start(bf16[3,256,256]{1,2,0:T(8,128)(2,1)S(1)} %pad_maximum_fusion.28), channel_id=1, source_target_pairs={{0,8},{4,12},{8,0},{12,4},{16,24},{20,28},{24,16},{28,20},{1,9},{5... | collective-permute-start | bytes 1179656 | tf_op jit(solution)/shard_map/ppermute | solution.py:44
  270.8 48.7 %collective-permute-start.31 = (bf16[512,768]{0,1:T(8,128)(2,1)S(1)}, bf16[512,768]{0,1:T(8,128)(2,1)S(1)}, u32[]{:S(2)}, u32[]{:S(2)}) collective-permute-start(bf16[512,768]{0,1:T(8,128)(2,1)S(1)} %pad_maximum_fusion.18), channel_id=1, source_target_pairs={{0,4},{4,0},{8,12},{12,8},{16,20},{20,16},{24,28},{28,24},{1,5},{5... | collective-permute-start | bytes 2359304 | tf_op jit(solution)/shard_map/ppermute | solution.py:44
  319.7 52.9 %collective-permute-start.35 = (bf16[1024,768]{0,1:T(8,128)(2,1)S(1)}, bf16[1024,768]{0,1:T(8,128)(2,1)S(1)}, u32[]{:S(2)}, u32[]{:S(2)}) collective-permute-start(bf16[1024,768]{0,1:T(8,128)(2,1)S(1)} %pad_maximum_fusion.6), channel_id=1, source_target_pairs={{0,2},{1,3},{2,0},{3,1},{4,6},{5,7},{6,4},{7,5},{8,10},{9,11},{10,... | collective-permute-start | bytes 4718600 | tf_op jit(solution)/shard_map/ppermute | solution.py:44
  406.6 49.5 %collective-permute-start.38 = (bf16[1024,1024]{1,0:T(8,128)(2,1)S(1)}, bf16[1024,1024]{1,0:T(8,128)(2,1)S(1)}, u32[]{:S(2)}, u32[]{:S(2)}) collective-permute-start(bf16[1024,1024]{1,0:T(8,128)(2,1)S(1)} %add_convert_fusion.8.refs_2_), channel_id=1, source_target_pairs={{0,1},{1,0},{2,3},{3,2},{4,5},{5,4},{6,7},{7,6},{8,9},{9,8},{10,11... | collective-permute-start | bytes 6291464 | tf_op jit(solution)/shard_map/ppermute | solution.py:44
  474.8 50.8 %collective-permute-start.46 = (bf16[1024,1024]{0,1:T(8,128)(2,1)S(1)}, bf16[1024,1024]{0,1:T(8,128)(2,1)S(1)}, u32[]{:S(2)}, u32[]{:S(2)}) collective-permute-start(bf16[1024,1024]{0,1:T(8,128)(2,1)S(1)} %pad_maximum_fusion.2), channel_id=1, source_target_pairs={{0,2},{1,3},{2,0},{3,1},{4,6},{5,7},{6,4},{7,5},{8,10},{9,11},{10,... | collective-permute-start | bytes 6291464 | tf_op jit(solution)/shard_map/ppermute | solution.py:44
  586.9 48.8 %collective-permute-start.87 = (bf16[1024,1024]{0,1:T(8,128)(2,1)}, bf16[1024,1024]{0,1:T(8,128)(2,1)}, u32[]{:S(2)}, u32[]{:S(2)}) collective-permute-start(bf16[1024,1024]{0,1:T(8,128)(2,1)} %convolution_convert_fusion), channel_id=1, source_target_pairs={{0,2},{1,3},{2,0},{3,1},{4,6},{5,7},{6,4},{7,5},{8,10},{9,11},{10,... | collective-permute-start | bytes 6291464 | tf_op jit(solution)/shard_map/ppermute | solution.py:44
  592.3 69.3 %collective-permute-start.78 = (bf16[512,1024]{0,1:T(8,128)(2,1)}, bf16[512,1024]{0,1:T(8,128)(2,1)}, u32[]{:S(2)}, u32[]{:S(2)}) collective-permute-start(bf16[512,1024]{0,1:T(8,128)(2,1)} %slice.1037), channel_id=1, source_target_pairs={{0,4},{4,0},{8,12},{12,8},{16,20},{20,16},{24,28},{28,24},{1,5},{5... | collective-permute-start | bytes 3145736 | tf_op jit(solution)/shard_map/ppermute | solution.py:44
  603.3 58.3 %collective-permute-start.80 = (bf16[512,1024]{0,1:T(8,128)(2,1)}, bf16[512,1024]{0,1:T(8,128)(2,1)}, u32[]{:S(2)}, u32[]{:S(2)}) collective-permute-start(bf16[512,1024]{0,1:T(8,128)(2,1)} %add_convert_fusion.14), channel_id=1, source_target_pairs={{0,2},{1,3},{2,0},{3,1},{4,6},{5,7},{6,4},{7,5},{8,10},{9,11},{10,... | collective-permute-start | bytes 3145736 | tf_op jit(solution)/shard_map/ppermute | solution.py:44
  679.9 75.7 %collective-permute-start.82 = (bf16[128,1024]{0,1:T(8,128)(2,1)}, bf16[128,1024]{0,1:T(8,128)(2,1)}, u32[]{:S(2)}, u32[]{:S(2)}) collective-permute-start(bf16[128,1024]{0,1:T(8,128)(2,1)} %add_convert_fusion.32), channel_id=1, source_target_pairs={{0,16},{4,20},{8,24},{12,28},{16,0},{20,4},{24,8},{28,12},{1,17},{... | collective-permute-start | bytes 786440 | tf_op jit(solution)/shard_map/ppermute | solution.py:44
  696.1 65.9 %collective-permute-start.90 = (bf16[128,1024]{0,1:T(8,128)(2,1)}, bf16[128,1024]{0,1:T(8,128)(2,1)}, u32[]{:S(2)}, u32[]{:S(2)}) collective-permute-start(bf16[128,1024]{0,1:T(8,128)(2,1)} %add_convert_fusion.30), channel_id=1, source_target_pairs={{0,16},{4,20},{8,24},{12,28},{16,0},{20,4},{24,8},{28,12},{1,17},{... | collective-permute-start | bytes 786440 | tf_op jit(solution)/shard_map/ppermute | solution.py:44
  728.8 56.3 %collective-permute-start.69 = (bf16[1024,768]{0,1:T(8,128)(2,1)}, bf16[1024,768]{0,1:T(8,128)(2,1)}, u32[]{:S(2)}, u32[]{:S(2)}) collective-permute-start(bf16[1024,768]{0,1:T(8,128)(2,1)} %pad_maximum_fusion.11), channel_id=1, source_target_pairs={{0,2},{1,3},{2,0},{3,1},{4,6},{5,7},{6,4},{7,5},{8,10},{9,11},{10,... | collective-permute-start | bytes 4718600 | tf_op jit(solution)/shard_map/ppermute | solution.py:44
  794.9 56.1 %collective-permute-start.64 = (bf16[128,768]{0,1:T(8,128)(2,1)}, bf16[128,768]{0,1:T(8,128)(2,1)}, u32[]{:S(2)}, u32[]{:S(2)}) collective-permute-start(bf16[128,768]{0,1:T(8,128)(2,1)} %add_convert_fusion.37), channel_id=1, source_target_pairs={{0,16},{4,20},{8,24},{12,28},{16,0},{20,4},{24,8},{28,12},{1,17},{... | collective-permute-start | bytes 589832 | tf_op jit(solution)/shard_map/ppermute | solution.py:44
  817.7 49.0 %collective-permute-start.74 = (bf16[512,1024]{0,1:T(8,128)(2,1)}, bf16[512,1024]{0,1:T(8,128)(2,1)}, u32[]{:S(2)}, u32[]{:S(2)}) collective-permute-start(bf16[512,1024]{0,1:T(8,128)(2,1)} %slice.1026), channel_id=1, source_target_pairs={{0,4},{4,0},{8,12},{12,8},{16,20},{20,16},{24,28},{28,24},{1,5},{5... | collective-permute-start | bytes 3145736 | tf_op jit(solution)/shard_map/ppermute | solution.py:44
  843.3 69.5 %collective-permute-start.73 = (bf16[512,1024]{0,1:T(8,128)(2,1)}, bf16[512,1024]{0,1:T(8,128)(2,1)}, u32[]{:S(2)}, u32[]{:S(2)}) collective-permute-start(bf16[512,1024]{0,1:T(8,128)(2,1)} %slice.1023), channel_id=1, source_target_pairs={{0,4},{4,0},{8,12},{12,8},{16,20},{20,16},{24,28},{28,24},{1,5},{5... | collective-permute-start | bytes 3145736 | tf_op jit(solution)/shard_map/ppermute | solution.py:44
  848.7 48.8 %collective-permute-start.83 = (bf16[1024,1024]{0,1:T(8,128)(2,1)}, bf16[1024,1024]{0,1:T(8,128)(2,1)}, u32[]{:S(2)}, u32[]{:S(2)}) collective-permute-start(bf16[1024,1024]{0,1:T(8,128)(2,1)} %convolution_convert_fusion.2), channel_id=1, source_target_pairs={{0,2},{1,3},{2,0},{3,1},{4,6},{5,7},{6,4},{7,5},{8,10},{9,11},{10,... | collective-permute-start | bytes 6291464 | tf_op jit(solution)/shard_map/ppermute | solution.py:44
  869.5 50.5 %collective-permute-start.75 = (bf16[512,1024]{0,1:T(8,128)(2,1)}, bf16[512,1024]{0,1:T(8,128)(2,1)}, u32[]{:S(2)}, u32[]{:S(2)}) collective-permute-start(bf16[512,1024]{0,1:T(8,128)(2,1)} %add_convert_fusion.15), channel_id=1, source_target_pairs={{0,2},{1,3},{2,0},{3,1},{4,6},{5,7},{6,4},{7,5},{8,10},{9,11},{10,... | collective-permute-start | bytes 3145736 | tf_op jit(solution)/shard_map/ppermute | solution.py:44
  892.1 62.8 %collective-permute-start.91 = (bf16[768,1024]{1,0:T(8,128)(2,1)}, bf16[768,1024]{1,0:T(8,128)(2,1)}, u32[]{:S(2)}, u32[]{:S(2)}) collective-permute-start(bf16[768,1024]{1,0:T(8,128)(2,1)} %convolution_convert_fusion.8), channel_id=1, source_target_pairs={{0,2},{1,3},{2,0},{3,1},{4,6},{5,7},{6,4},{7,5},{8,10},{9,11},{10,... | collective-permute-start | bytes 4718600 | tf_op jit(solution)/shard_map/ppermute | solution.py:44
  909.6 60.5 %collective-permute-start.54 = (bf16[1024,1024]{1,0:T(8,128)(2,1)S(1)}, bf16[1024,1024]{1,0:T(8,128)(2,1)}, u32[]{:S(2)}, u32[]{:S(2)}) collective-permute-start(bf16[1024,1024]{1,0:T(8,128)(2,1)S(1)} %add_convert_fusion.1.refs_2_), channel_id=1, source_target_pairs={{0,1},{1,0},{2,3},{3,2},{4,5},{5,4},{6,7},{7,6},{8,9},{9,8},{10,11... | collective-permute-start | bytes 6291464 | tf_op jit(solution)/shard_map/ppermute | solution.py:44
  957.4 75.5 %collective-permute-start.92 = (bf16[384,1024]{1,0:T(8,128)(2,1)}, bf16[384,1024]{1,0:T(8,128)(2,1)S(1)}, u32[]{:S(2)}, u32[]{:S(2)}) collective-permute-start(bf16[384,1024]{1,0:T(8,128)(2,1)} %add_convert_fusion.16), channel_id=1, source_target_pairs={{0,4},{4,0},{8,12},{12,8},{16,20},{20,16},{24,28},{28,24},{1,5},{5... | collective-permute-start | bytes 2359304 | tf_op jit(solution)/shard_map/ppermute | solution.py:44
  1003.3 55.3 %collective-permute-start.65 = (bf16[1024,768]{0,1:T(8,128)(2,1)}, bf16[1024,768]{0,1:T(8,128)(2,1)}, u32[]{:S(2)}, u32[]{:S(2)}) collective-permute-start(bf16[1024,768]{0,1:T(8,128)(2,1)} %pad_maximum_fusion.9), channel_id=1, source_target_pairs={{0,2},{1,3},{2,0},{3,1},{4,6},{5,7},{6,4},{7,5},{8,10},{9,11},{10,... | collective-permute-start | bytes 4718600 | tf_op jit(solution)/shard_map/ppermute | solution.py:44
  (330 other events, 6471.3 us)
Sparse Core Ops, SparseCore 0:
  25.7 34.1 all-reduce.2

commit v2 on v1

v2 whole, which is shorter than its diff:
```python
import functools
import math

import jax
import jax.numpy as jnp
from jax import lax
from jax.experimental import pallas as pl
from jax.experimental.pallas import tpu as pltpu
from jax.sharding import Mesh
from jax.sharding import PartitionSpec as P

HEAD_DIM = 64
STEP = 10
LANES = 128

QKV, MID, TEXT, UP, DOWN, SMALL = range(6)
GRAD = 10
START, DONE = range(2)
(
    AT_ATTEND,
    AT_ATTEND_NEXT,
    AT_ATTENDED,
    AT_CROSS,
    AT_CROSSED,
    AT_ACTIVE,
    AT_MLP,
    AT_HIDDEN_GRAD,
    AT_MLP_GRAD,
    AT_CROSS_GRAD,
    AT_CROSSED_GRAD,
    AT_SELF_GRAD,
    AT_SELF_GRAD_NEXT,
    AT_ATTENDED_GRAD,
) = range(14)
FULL, NEAR, ALONG_DP = range(3)
ACROSS, BESIDE, CORNER = range(100, 103)
DP, ITEM, RANK = "dp", "item", "rank"
MODEL = (ITEM, RANK)

norm_eps = 1e-06
clip_limit = 0.001
matrix_rate = 0.04
gain_rate = 0.6
row_rate = 0.1
beta_first = 0.9
beta_second = 0.999
adam_eps = 1e-08
weight_decay = 0.01
average_keep = 0.5
snr_limit = 5.0

score_scale = HEAD_DIM ** (-0.5)
log2_e = 1.4426950408889634
exp_scale = score_scale * log2_e
masked_score = -1e30


def as_low(tensor):
    return tensor.astype(jnp.bfloat16)


def plan():
    beta_table = jnp.linspace(0.00085**0.5, 0.012**0.5, 1000, dtype=jnp.float32) ** 2
    return jnp.cumprod(1.0 - beta_table)


def exchange(tensor, axis, mask):
    size = lax.axis_size(axis)
    return lax.ppermute(tensor, axis, [(i, i ^ mask) for i in range(size)])


class Layout:
    def __init__(self):
        self.dp_size = lax.axis_size(DP)
        self.items = lax.axis_size(ITEM)
        self.ranks = lax.axis_size(RANK)
        self.dp = lax.axis_index(DP)
        self.item = lax.axis_index(ITEM)
        self.rank = lax.axis_index(RANK)
        self.masks = []
        mask = self.dp_size >> 1
        while mask:
            self.masks.append(mask)
            mask >>= 1
        self.offsets = [
            sum(mask for bit, mask in enumerate(self.masks) if (place >> bit) & 1)
            for place in range(self.dp_size)
        ]

    def blocks(self):
        return jnp.bitwise_xor(self.dp, jnp.array(self.offsets, jnp.int32))

    def other_item(self, tensor):
        return exchange(tensor, ITEM, 1)


def gather_dp(layout, part, axis, masks, stages=None):
    for mask in masks:
        part = jnp.concatenate([part, exchange(part, DP, mask)], axis)
        if stages is not None:
            stages.append(part)
    return part


def nothing_kernel(*refs):
    pass


def checkpoint(values, waits):
    anywhere = pl.BlockSpec(memory_space=pl.ANY)
    return pl.pallas_call(
        nothing_kernel,
        in_specs=[anywhere] * (len(values) + len(waits)),
        out_specs=[anywhere] * len(values),
        out_shape=[jax.ShapeDtypeStruct(value.shape, value.dtype) for value in values],
        input_output_aliases={index: index for index in range(len(values))},
        cost_estimate=pl.CostEstimate(flops=0, bytes_accessed=0, transcendentals=0),
        name="checkpoint",
    )(*values, *waits)


class Gather:
    def __init__(self, layout, near, axis, first_dp, early):
        self.layout, self.near, self.axis, self.first_dp = layout, near, axis, first_dp
        self.early = early
        self.received = []

    def count(self):
        return len(self.early) + 2

    def source(self, place):
        while len(self.received) < place:
            self.send(len(self.received), self.source(len(self.received)))
        planes = place - len(self.early)
        if planes == 1:
            return self.beside if self.first_dp else self.across
        if planes < 0 and place > 0 or planes == 0 and self.early:
            self.near = jnp.concatenate([self.near, self.received[-1]], self.axis)
        return self.near

    def send(self, place, tensor):
        planes = place - len(self.early)
        if planes < 0:
            self.near = tensor
            self.received.append(exchange(tensor, DP, self.early[place]))
        elif planes == 0:
            self.near = tensor
            self.across = exchange(tensor, DP, self.layout.masks[-1])
            self.beside = self.layout.other_item(tensor)
            self.received.append((self.across, self.beside))
        else:
            if self.first_dp:
                self.beside = tensor
                self.corner = exchange(tensor, DP, self.layout.masks[-1])
            else:
                self.across = tensor
                self.corner = self.layout.other_item(tensor)
            self.received.append(self.corner)

    def finish(self):
        while len(self.received) < self.count():
            self.send(len(self.received), self.source(len(self.received)))
        return [
            jnp.concatenate([self.near, self.across], self.axis),
            jnp.concatenate([self.beside, self.corner], self.axis),
        ]


class Scatter:
    def __init__(self, layout, pair, first_dp):
        self.layout, self.first_dp, self.kind = layout, first_dp, pair[0].dtype
        half = pair[0].shape[0] // 2
        (self.near, across), (beside, self.corner) = [
            (part[:half], part[half:]) for part in pair
        ]
        self.second, self.third = (across, beside) if first_dp else (beside, across)
        self.masks = list(reversed(layout.masks[:-1]))
        self.received = []

    def count(self):
        return 3 + len(self.masks)

    def source(self, place):
        while 1 < place > len(self.received):
            self.send(len(self.received), self.source(len(self.received)))
        if place == 0:
            return self.corner
        if place == 1:
            return self.second
        if place == 2:
            return add_terms([self.third, self.received[0]]).astype(self.kind)
        if place == 3:
            self.terms = [self.near, self.received[1], self.received[2]]
        else:
            self.terms = self.terms + [self.received[-1]]
        half = self.terms[0].shape[0] // 2
        passed = add_terms([term[half:] for term in self.terms]).astype(self.kind)
        self.terms = [term[:half] for term in self.terms]
        return passed

    def send(self, place, tensor):
        if place > 2:
            moved = exchange(tensor, DP, self.masks[place - 3])
        elif self.first_dp == (place < 2):
            moved = exchange(tensor, DP, self.layout.masks[-1])
        else:
            moved = self.layout.other_item(tensor)
        self.received.append(moved)

    def finish(self):
        while len(self.received) < self.count():
            self.send(len(self.received), self.source(len(self.received)))
        return add_terms(self.terms + [self.received[-1]])


class Flow:
    def __init__(self):
        self.chunks = {}

    def add(self, name, chunk):
        self.chunks[name] = chunk
        return chunk

    def at(self, point, values):
        starts, sources, waits = [], [], []
        for action, name, level, place in flow_table.get(point, ()):
            chunk = self.chunks.get((name, level))
            if chunk is None:
                continue
            place = place if place >= 0 else chunk.count() + place
            if action == START and place >= len(chunk.received):
                starts.append((chunk, place))
                sources.append(chunk.source(place))
            elif action == DONE and place < len(chunk.received):
                got = chunk.received[place]
                waits.extend(got if isinstance(got, tuple) else [got])
        if not sources and not waits:
            return list(values)
        waits = [wait for wait in waits if all(wait is not source for source in sources)]
        result = checkpoint(list(values) + sources, waits)
        for (chunk, place), source in zip(starts, result[len(values) :]):
            chunk.send(place, source)
        return list(result[: len(values)])


class Chunk:
    def __init__(self, shape, mode, first_dp=False):
        self.shape, self.mode, self.first_dp = shape, mode, first_dp

    def out_shape(self, dp_size):
        lead = {FULL: (2, dp_size), NEAR: (dp_size // 2,), ALONG_DP: (dp_size,)}[self.mode]
        return jax.ShapeDtypeStruct(lead + self.shape, jnp.bfloat16)


def gather_order(chunks, levels):
    pending, finish = [], {}
    for index, chunk in enumerate(chunks):
        unit = chunk.shape[-1] * math.prod(chunk.shape[:-1])
        before = []
        for stage in range(levels - 1):
            cost = unit * 2**stage * (2 if stage == 0 else 1)
            pending.append((index, stage, NEAR, before, cost))
            before = before + [stage]
        block = unit * 2 ** (levels - 1)
        if chunk.mode in (FULL, ALONG_DP):
            pending.append((index, ACROSS, ACROSS, before, block))
        if chunk.mode == FULL:
            pending.append((index, BESIDE, BESIDE, before, block))
            link, need = (ACROSS, BESIDE) if chunk.first_dp else (BESIDE, ACROSS)
            pending.append((index, CORNER, link, before + [need], block))
    order, free = [], {}
    while pending:
        best = None
        for entry in pending:
            index, name, link, needs, cost = entry
            if any((index, need) not in finish for need in needs):
                continue
            ready = max([finish[index, need] for need in needs] + [0])
            start = max(free.get(link, 0), ready)
            if best is None or (start, index) < best[0]:
                best = ((start, index), entry)
        (start, _), entry = best
        index, name, link, needs, cost = entry
        free[link] = start + cost
        finish[index, name] = start + cost + 100000
        order.append(entry[:4])
        pending.remove(entry)
    return order


def gather_kernel(masks, chunks, *refs):
    count = len(chunks)
    shards, outs = refs[:count], refs[count : 2 * count]
    local_sems, send_sems, recv_sems = refs[2 * count :]
    dp, item, rank = (lax.axis_index(name) for name in (DP, ITEM, RANK))
    levels = len(masks)
    half = 2 ** (levels - 1)
    dp_peers = [{DP: jnp.bitwise_xor(dp, mask), ITEM: item, RANK: rank} for mask in masks]
    item_peer = {DP: dp, ITEM: 1 - item, RANK: rank}

    barrier = pltpu.get_barrier_semaphore()
    for peer in dp_peers + [item_peer]:
        pl.semaphore_signal(barrier, inc=1, device_id=peer, device_id_type=pl.DeviceIdType.MESH)
    pl.semaphore_wait(barrier, levels + 1)

    own = []
    for index, chunk in enumerate(chunks):
        place = outs[index].at[0, 0] if chunk.mode == FULL else outs[index].at[0]
        own.append(pltpu.make_async_copy(shards[index], place, local_sems.at[index]))
        own[-1].start()

    def transfer(index, name):
        chunk, out = chunks[index], outs[index]
        mine = out.at[0] if chunk.mode == FULL else out
        if name < ACROSS:
            stage = name
            size = 2**stage
            source, target = mine.at[pl.ds(0, size)], mine.at[pl.ds(size, size)]
            if stage == 0:
                source, target = shards[index], mine.at[1]
            return source, target, dp_peers[stage]
        if name == ACROSS:
            return mine.at[pl.ds(0, half)], mine.at[pl.ds(half, half)], dp_peers[-1]
        theirs = out.at[1]
        if name == BESIDE:
            return mine.at[pl.ds(0, half)], theirs.at[pl.ds(0, half)], item_peer
        if chunk.first_dp:
            return theirs.at[pl.ds(0, half)], theirs.at[pl.ds(half, half)], dp_peers[-1]
        return mine.at[pl.ds(half, half)], theirs.at[pl.ds(half, half)], item_peer

    copies, arrived, placed = {}, set(), set()
    for number, (index, name, _, needs) in enumerate(gather_order(chunks, levels)):
        for need in needs:
            if (index, need) not in arrived:
                arrived.add((index, need))
                copies[index, need].wait_recv()
        if needs and index not in placed:
            placed.add(index)
            own[index].wait()
        source, target, peer = transfer(index, name)
        copy = pltpu.make_async_remote_copy(
            src_ref=source,
            dst_ref=target,
            send_sem=send_sems.at[number],
            recv_sem=recv_sems.at[number],
            device_id=peer,
            device_id_type=pl.DeviceIdType.MESH,
        )
        copy.start()
        copies[index, name] = copy
    for index in range(count):
        if index not in placed:
            own[index].wait()
    for key, copy in copies.items():
        if key not in arrived:
            copy.wait_recv()
    for copy in copies.values():
        copy.wait_send()


def gather_first(layout, shards, chunks, waits):
    transfers = len(gather_order(chunks, len(layout.masks)))
    return pl.pallas_call(
        after(len(waits), functools.partial(gather_kernel, layout.masks, chunks)),
        in_specs=[pl.BlockSpec(memory_space=pl.ANY)] * (len(waits) + len(chunks)),
        out_specs=[pl.BlockSpec(memory_space=pl.ANY)] * len(chunks),
        out_shape=[chunk.out_shape(layout.dp_size) for chunk in chunks],
        scratch_shapes=[
            pltpu.SemaphoreType.DMA((len(chunks),)),
            pltpu.SemaphoreType.DMA((transfers,)),
            pltpu.SemaphoreType.DMA((transfers,)),
        ],
        compiler_params=pltpu.CompilerParams(
            collective_id=1, has_side_effects=True, vmem_limit_bytes=16 * 2**20
        ),
        cost_estimate=pl.CostEstimate(flops=10000, bytes_accessed=10**8, transcendentals=0),
        name="gather_first",
    )(*waits, *shards)


def add_terms(terms):
    total = terms[0].astype(jnp.float32)
    for term in terms[1:]:
        total = total + term.astype(jnp.float32)
    return total


def totals_kernel(value_ref, out_ref, rank_slots, dp_slots, rank_sems, dp_sems):
    dp, item, rank = (lax.axis_index(name) for name in (DP, ITEM, RANK))
    dp_size, ranks = lax.axis_size(DP), lax.axis_size(RANK)
    group = lax.axis_size(ITEM) * ranks
    me = item * ranks + rank
    group_ids, dp_ids = [], []
    for step in range(1, group):
        peer = lax.rem(me + step, group)
        group_ids.append({DP: dp, ITEM: peer // ranks, RANK: lax.rem(peer, ranks)})
    for step in range(1, dp_size):
        dp_ids.append({DP: lax.rem(dp + step, dp_size), ITEM: item, RANK: rank})
    barrier = pltpu.get_barrier_semaphore()
    for peer in group_ids + dp_ids:
        pl.semaphore_signal(barrier, inc=1, device_id=peer, device_id_type=pl.DeviceIdType.MESH)
    pl.semaphore_wait(barrier, len(group_ids) + len(dp_ids))

    def share(place, slots, sems, peers):
        copies = []
        for step, peer in enumerate(peers):
            copies.append(
                pltpu.make_async_remote_copy(
                    src_ref=slots.at[place],
                    dst_ref=slots.at[place],
                    send_sem=sems.at[0, step],
                    recv_sem=sems.at[1, step],
                    device_id=peer,
                    device_id_type=pl.DeviceIdType.MESH,
                )
            )
            copies[-1].start()
        for copy in copies:
            copy.wait()
        total = slots[0]
        for index in range(1, len(peers) + 1):
            total = total + slots[index]
        return total

    rank_slots[me] = value_ref[...]
    dp_slots[dp] = share(me, rank_slots, rank_sems, group_ids)
    out_ref[...] = share(dp, dp_slots, dp_sems, dp_ids)


def all_totals(layout, values):
    tile = jnp.zeros((8, LANES), jnp.float32).at[0, : values.shape[0]].set(values)
    group = layout.items * layout.ranks
    total = pl.pallas_call(
        totals_kernel,
        in_specs=[pl.BlockSpec(memory_space=pltpu.VMEM)],
        out_specs=pl.BlockSpec(memory_space=pltpu.VMEM),
        out_shape=jax.ShapeDtypeStruct(tile.shape, jnp.float32),
        scratch_shapes=[
            pltpu.VMEM((group,) + tile.shape, jnp.float32),
            pltpu.VMEM((layout.dp_size,) + tile.shape, jnp.float32),
            pltpu.SemaphoreType.DMA((2, group - 1)),
            pltpu.SemaphoreType.DMA((2, layout.dp_size - 1)),
        ],
        compiler_params=pltpu.CompilerParams(collective_id=0, has_side_effects=True),
        cost_estimate=pl.CostEstimate(flops=10000, bytes_accessed=100000, transcendentals=0),
        name="totals",
    )(tile)
    return total[0, : values.shape[0]]


def swapped_sum(part_ref, own_ref, slots, send_sems, recv_sems):
    ranks = lax.axis_size(RANK)
    dp, item, rank = (lax.axis_index(name) for name in (DP, ITEM, RANK))
    step, steps = pl.program_id(0), part_ref.shape[0] // own_ref.shape[0]
    rows = own_ref.shape[0]
    place = 0 if ranks == 2 else rank
    peers = [
        {DP: dp, ITEM: item, RANK: lax.rem(rank + ahead, ranks)} for ahead in range(1, ranks)
    ]

    def copies(chunk):
        span = pl.ds(pl.multiple_of(chunk * rows, rows), rows)
        return [
            pltpu.make_async_remote_copy(
                src_ref=part_ref.at[span],
                dst_ref=slots.at[place, span],
                send_sem=send_sems.at[index, chunk],
                recv_sem=recv_sems.at[index, chunk],
                device_id=peer,
                device_id_type=pl.DeviceIdType.MESH,
            )
            for index, peer in enumerate(peers)
        ]

    @pl.when(step == 0)
    def _():
        barrier = pltpu.get_barrier_semaphore()
        for peer in peers:
            pl.semaphore_signal(
                barrier, inc=1, device_id=peer, device_id_type=pl.DeviceIdType.MESH
            )
        pl.semaphore_wait(barrier, len(peers))
        for chunk in range(steps):
            for copy in copies(chunk):
                copy.start()

    for copy in copies(step):
        copy.wait_recv()
    span = pl.ds(pl.multiple_of(step * rows, rows), rows)
    if ranks == 2:
        total = own_ref[...].astype(jnp.float32) + slots[0, span].astype(jnp.float32)
    else:
        slots[rank, span] = own_ref[...]
        total = add_terms([slots[index, span] for index in range(ranks)])

    @pl.when(step == steps - 1)
    def _():
        for chunk in range(steps):
            for copy in copies(chunk):
                copy.wait_send()

    return total


def swap_scratch(ranks, frames, rows, width):
    return [
        pltpu.VMEM((1 if ranks == 2 else ranks, frames, width), jnp.bfloat16),
        pltpu.SemaphoreType.DMA((ranks - 1, frames // rows)),
        pltpu.SemaphoreType.DMA((ranks - 1, frames // rows)),
    ]


def normalise(resid):
    centre = resid - jnp.mean(resid, -1, keepdims=True)
    inverse = lax.rsqrt(jnp.mean(centre * centre, -1, keepdims=True) + norm_eps)
    return (centre * inverse, inverse)


def norm_forward_kernel(resid_ref, gain_ref, low_ref):
    low_ref[...] = (normalise(resid_ref[...])[0] * gain_ref[...]).astype(jnp.bfloat16)


def norm_swap_forward_kernel(part_ref, own_ref, resid_ref, gain_ref, out_ref, low_ref, *swap):
    resid = resid_ref[...] + swapped_sum(part_ref, own_ref, *swap)
    out_ref[...] = resid
    low_ref[...] = (normalise(resid)[0] * gain_ref[...]).astype(jnp.bfloat16)


def norm_forward(resid, gain, part=None):
    frames, width = resid.shape
    rows = min(256, frames)
    block = pl.BlockSpec((rows, width), lambda i: (i, 0))
    gain_block = pl.BlockSpec((1, width), lambda i: (0, 0))
    low_shape = jax.ShapeDtypeStruct((frames, width), jnp.bfloat16)
    cost = pl.CostEstimate(
        flops=10 * frames * width, bytes_accessed=14 * frames * width, transcendentals=0
    )
    if part is None:
        return (
            resid,
            pl.pallas_call(
                norm_forward_kernel,
                grid=(frames // rows,),
                in_specs=[block, gain_block],
                out_specs=block,
                out_shape=low_shape,
                cost_estimate=cost,
                compiler_params=pltpu.CompilerParams(vmem_limit_bytes=32 * 2**20),
                name="norm_fwd",
            )(resid, gain[None]),
        )
    return pl.pallas_call(
        norm_swap_forward_kernel,
        grid=(frames // rows,),
        in_specs=[pl.BlockSpec(memory_space=pl.ANY), block, block, gain_block],
        out_specs=[block, block],
        out_shape=[jax.ShapeDtypeStruct((frames, width), jnp.float32), low_shape],
        scratch_shapes=swap_scratch(lax.axis_size(RANK), frames, rows, width),
        cost_estimate=cost,
        compiler_params=pltpu.CompilerParams(
            collective_id=2, has_side_effects=True, vmem_limit_bytes=32 * 2**20
        ),
        name="norm_swap_fwd",
    )(part, part, resid, gain[None])


def norm_step(resid, gain, upstream):
    normed, inverse = normalise(resid)
    scaled = upstream * gain
    step = inverse * (
        scaled
        - jnp.mean(scaled, -1, keepdims=True)
        - normed * jnp.mean(scaled * normed, -1, keepdims=True)
    )
    rows, width = resid.shape
    return (step, jnp.sum((upstream * normed).reshape(rows // 8, 8, width), axis=0))


def add_gain_term(gain_grad_ref, term):
    @pl.when(pl.program_id(0) == 0)
    def _():
        gain_grad_ref[...] = term

    @pl.when(pl.program_id(0) > 0)
    def _():
        gain_grad_ref[...] = gain_grad_ref[...] + term


def norm_backward_kernel(upstream_ref, resid_ref, gain_ref, out_ref, low_ref, gain_grad_ref):
    step, term = norm_step(resid_ref[...], gain_ref[...], upstream_ref[...])
    out_ref[...] = step
    low_ref[...] = step.astype(jnp.bfloat16)
    add_gain_term(gain_grad_ref, term)


def norm_swap_backward_kernel(
    part_ref, own_ref, resid_ref, gain_ref, grad_ref, out_ref, low_ref, gain_grad_ref, *swap
):
    upstream = swapped_sum(part_ref, own_ref, *swap)
    step, term = norm_step(resid_ref[...], gain_ref[...], upstream)
    step = grad_ref[...] + step
    out_ref[...] = step
    low_ref[...] = step.astype(jnp.bfloat16)
    add_gain_term(gain_grad_ref, term)


def norm_backward(resid, gain, upstream, resid_grad=None, waits=()):
    frames, width = resid.shape
    rows = min(256, frames)
    block = pl.BlockSpec((rows, width), lambda i: (i, 0))
    gain_block = pl.BlockSpec((1, width), lambda i: (0, 0))
    out_specs = [block, block, pl.BlockSpec((8, width), lambda i: (0, 0))]
    out_shape = [
        jax.ShapeDtypeStruct((frames, width), jnp.float32),
        jax.ShapeDtypeStruct((frames, width), jnp.bfloat16),
        jax.ShapeDtypeStruct((8, width), jnp.float32),
    ]
    cost = pl.CostEstimate(
        flops=20 * frames * width, bytes_accessed=18 * frames * width, transcendentals=0
    )
    if resid_grad is None:
        result = pl.pallas_call(
            norm_backward_kernel,
            grid=(frames // rows,),
            in_specs=[block, block, gain_block],
            out_specs=out_specs,
            out_shape=out_shape,
            cost_estimate=cost,
            compiler_params=pltpu.CompilerParams(vmem_limit_bytes=40 * 2**20),
            name="norm_bwd",
        )(upstream, resid, gain[None])
    else:
        result = pl.pallas_call(
            after(len(waits), norm_swap_backward_kernel),
            grid=(frames // rows,),
            in_specs=[pl.BlockSpec(memory_space=pl.ANY)] * (len(waits) + 1)
            + [block, block, gain_block, block],
            out_specs=out_specs,
            out_shape=out_shape,
            scratch_shapes=swap_scratch(lax.axis_size(RANK), frames, rows, width),
            cost_estimate=cost,
            compiler_params=pltpu.CompilerParams(
                collective_id=4 if waits else 3, has_side_effects=True, vmem_limit_bytes=40 * 2**20
            ),
            name="norm_swap_bwd",
        )(*waits, upstream, upstream, resid, gain[None], resid_grad)
    return (result[0], result[1], jnp.sum(result[2], 0))


def after(count, kernel):
    return lambda *refs: kernel(*refs[count:])


def dot_nt(left, right):
    return lax.dot_general(
        left, right, (((1,), (1,)), ((), ())), preferred_element_type=jnp.float32
    )


def dot_nn(left, right):
    return jnp.dot(left, right, preferred_element_type=jnp.float32)


def head_lanes(block, head):
    lane = lax.broadcasted_iota(jnp.int32, block.shape, 1)
    keep = lane >= HEAD_DIM if head else lane < HEAD_DIM
    return jnp.where(keep, block, jnp.zeros_like(block))


def attend_forward_kernel(masked, len_ref, q_ref, k_ref, v_ref, out_ref, log_ref):
    queries, keys_in = q_ref[...], k_ref[...]
    values_t = v_ref[...].T
    outputs = []
    for head in range(2):
        scores = dot_nt(keys_in, head_lanes(queries, head))
        if masked:
            place = lax.broadcasted_iota(jnp.int32, scores.shape, 0)
            scores = jnp.where(place < len_ref[0], scores, masked_score)
        largest = jnp.max(scores, 0, keepdims=True)
        exp_scores = jnp.exp2((scores - largest) * exp_scale)
        totals = jnp.sum(exp_scores, 0, keepdims=True)
        part = dot_nn(
            values_t[head * HEAD_DIM : (head + 1) * HEAD_DIM], exp_scores.astype(jnp.bfloat16)
        )
        outputs.append(part / totals)
        log_ref[0, head : head + 1, :] = largest * exp_scale + jnp.log2(totals)
    out_ref[...] = jnp.concatenate(outputs, 0).T.astype(jnp.bfloat16)


def attend_forward(lengths, queries, q_at, keys_in, k_at, values_in, v_at, width, masked, waits=()):
    frames, keys = queries.shape[0], keys_in.shape[0]
    rows = min(256, frames)
    pairs = width // LANES
    q_at, k_at, v_at = q_at // LANES, k_at // LANES, v_at // LANES
    return pl.pallas_call(
        after(len(waits), functools.partial(attend_forward_kernel, masked)),
        grid=(pairs, frames // rows),
        in_specs=[pl.BlockSpec(memory_space=pl.ANY)] * len(waits)
        + [
            pl.BlockSpec(memory_space=pltpu.SMEM),
            pl.BlockSpec((rows, LANES), lambda p, i: (i, q_at + p)),
            pl.BlockSpec((keys, LANES), lambda p, i: (0, k_at + p)),
            pl.BlockSpec((keys, LANES), lambda p, i: (0, v_at + p)),
        ],
        out_specs=[
            pl.BlockSpec((rows, LANES), lambda p, i: (i, p)),
            pl.BlockSpec((1, 8, rows), lambda p, i: (p, 0, i)),
        ],
        out_shape=[
            jax.ShapeDtypeStruct((frames, width), jnp.bfloat16),
            jax.ShapeDtypeStruct((pairs, 8, frames), jnp.float32),
        ],
        cost_estimate=pl.CostEstimate(
            flops=16 * width * frames * keys,
            bytes_accessed=8 * frames * width,
            transcendentals=frames * keys * width // HEAD_DIM,
        ),
        compiler_params=pltpu.CompilerParams(vmem_limit_bytes=40 * 2**20),
        name="attend_fwd",
    )(*waits, lengths, queries, keys_in, values_in)


def attend_backward_kernel(
    masked, split, len_ref, q_ref, k_ref, v_ref, o_ref, g_ref, log_ref, *refs
):
    if split:
        dq_ref, dkv_ref, dk_acc, dv_acc, keys_t = refs
    else:
        dkv_ref, dk_acc, dv_acc, keys_t = refs
    pair, step = pl.program_id(0), pl.program_id(1)
    queries, keys_in, values_in = q_ref[...], k_ref[...], v_ref[...]
    out_grad = g_ref[...]
    rows = queries.shape[0]

    @pl.when(step == 0)
    def _():
        keys_t[...] = keys_in.T

    product = (out_grad.astype(jnp.float32) * o_ref[...].astype(jnp.float32)).T
    probs, grads, q_heads, g_heads, dq_parts = [], [], [], [], []
    for head in range(2):
        q_head, g_head = head_lanes(queries, head), head_lanes(out_grad, head)
        span = slice(head * HEAD_DIM, (head + 1) * HEAD_DIM)
        scores = dot_nt(keys_in, q_head) * exp_scale - log_ref[0, head : head + 1, :]
        if masked:
            place = lax.broadcasted_iota(jnp.int32, scores.shape, 0)
            scores = jnp.where(place < len_ref[0], scores, masked_score)
        prob = jnp.exp2(scores)
        delta = jnp.sum(product[span], 0, keepdims=True)
        grad = (prob * (dot_nt(values_in, g_head) - delta)).astype(jnp.bfloat16)
        dq_parts.append(dot_nn(keys_t[span, :], grad))
        probs.append(prob.astype(jnp.bfloat16))
        grads.append(grad)
        q_heads.append(q_head)
        g_heads.append(g_head)
    dq = (jnp.concatenate(dq_parts, 0) * score_scale).T.astype(jnp.bfloat16)
    dk = dot_nn(jnp.concatenate(grads, 1), jnp.concatenate(q_heads, 0))
    dv = dot_nn(jnp.concatenate(probs, 1), jnp.concatenate(g_heads, 0))
    width = dkv_ref.shape[1] // (2 if split else 3)
    place = pl.multiple_of(pair * LANES, LANES)
    if split:
        dq_ref[...] = dq
        k_at, v_at = place, place + width
    else:
        dkv_ref[pl.ds(pl.multiple_of(step * rows, rows), rows), pl.ds(place, LANES)] = dq
        k_at, v_at = place + width, place + 2 * width

    @pl.when(step == 0)
    def _():
        dk_acc[...] = dk
        dv_acc[...] = dv

    @pl.when(step > 0)
    def _():
        dk_acc[...] = dk_acc[...] + dk
        dv_acc[...] = dv_acc[...] + dv

    @pl.when(step == pl.num_programs(1) - 1)
    def _():
        dkv_ref[:, pl.ds(pl.multiple_of(k_at, LANES), LANES)] = (
            dk_acc[...] * score_scale
        ).astype(jnp.bfloat16)
        dkv_ref[:, pl.ds(pl.multiple_of(v_at, LANES), LANES)] = dv_acc[...].astype(jnp.bfloat16)


def attend_backward(
    lengths, queries, q_at, keys_in, k_at, values_in, v_at, outputs, out_grad, logs, width, split, waits=()
):
    frames, keys = queries.shape[0], keys_in.shape[0]
    rows = min(256, frames)
    pairs = width // LANES
    q_at, k_at, v_at = q_at // LANES, k_at // LANES, v_at // LANES
    row_block = pl.BlockSpec((rows, LANES), lambda p, i: (i, p))
    outs = [jax.ShapeDtypeStruct((keys, width * (2 if split else 3)), jnp.bfloat16)]
    out_specs = [pl.BlockSpec(outs[0].shape, lambda p, i: (0, 0))]
    if split:
        outs = [jax.ShapeDtypeStruct((frames, width), jnp.bfloat16)] + outs
        out_specs = [row_block] + out_specs
    return pl.pallas_call(
        after(len(waits), functools.partial(attend_backward_kernel, split, split)),
        grid=(pairs, frames // rows),
        in_specs=[pl.BlockSpec(memory_space=pl.ANY)] * len(waits)
        + [
            pl.BlockSpec(memory_space=pltpu.SMEM),
            pl.BlockSpec((rows, LANES), lambda p, i: (i, q_at + p)),
            pl.BlockSpec((keys, LANES), lambda p, i: (0, k_at + p)),
            pl.BlockSpec((keys, LANES), lambda p, i: (0, v_at + p)),
            row_block,
            row_block,
            pl.BlockSpec((1, 8, rows), lambda p, i: (p, 0, i)),
        ],
        out_specs=out_specs,
        out_shape=outs,
        scratch_shapes=[
            pltpu.VMEM((keys, LANES), jnp.float32),
            pltpu.VMEM((keys, LANES), jnp.float32),
            pltpu.VMEM((LANES, keys), jnp.bfloat16),
        ],
        cost_estimate=pl.CostEstimate(
            flops=40 * width * frames * keys,
            bytes_accessed=16 * frames * width,
            transcendentals=frames * keys * width // HEAD_DIM,
        ),
        compiler_params=pltpu.CompilerParams(vmem_limit_bytes=48 * 2**20),
        name="attend_bwd",
    )(*waits, lengths, queries, keys_in, values_in, outputs, out_grad, logs)


flow_table = {
    (AT_ATTENDED, 0): [
        (DONE, UP, 0, 0),
        (DONE, DOWN, 0, 0),
        (DONE, UP, 1, 0),
        (DONE, DOWN, 1, 0),
        (START, UP, 0, 1),
        (START, DOWN, 0, 1),
        (START, UP, 1, 1),
        (START, DOWN, 1, 1),
    ],
    (AT_CROSSED, 0): [
        (DONE, UP, 0, 1),
        (DONE, DOWN, 0, 1),
        (DONE, UP, 1, 1),
        (DONE, DOWN, 1, 1),
        (START, QKV, 1, 0),
        (START, MID, 1, 0),
    ],
    (AT_MLP, 0): [
        (DONE, QKV, 1, 0),
        (DONE, MID, 1, 0),
        (START, QKV, 1, 1),
        (START, MID, 1, 1),
    ],
    (AT_ATTEND, 1): [
        (DONE, MID, 1, 1),
        (START, UP, 1, 2),
        (START, DOWN, 1, 2),
    ],
    (AT_CROSS, 1): [
        (DONE, UP, 1, 2),
        (DONE, DOWN, 1, 2),
        (START, UP, 1, 3),
        (START, DOWN, 1, 3),
    ],
    (AT_HIDDEN_GRAD, 1): [(START, GRAD + DOWN, 1, 0)],
    (AT_MLP_GRAD, 1): [(START, GRAD + DOWN, 1, 1), (START, GRAD + UP, 1, 0)],
    (AT_CROSS_GRAD, 1): [
        (DONE, GRAD + DOWN, 1, 0),
        (START, GRAD + DOWN, 1, 2),
        (START, GRAD + UP, 1, 1),
    ],
    (AT_CROSSED_GRAD, 1): [
        (DONE, GRAD + DOWN, 1, 1),
        (DONE, GRAD + UP, 1, 0),
        (START, GRAD + UP, 1, 2),
    ],
    (AT_SELF_GRAD, 1): [(DONE, GRAD + UP, 1, 1), (START, GRAD + MID, 1, 0)],
    (AT_SELF_GRAD_NEXT, 1): [
        (DONE, GRAD + DOWN, 1, 2),
        (DONE, GRAD + UP, 1, 2),
        (START, GRAD + DOWN, 1, 3),
        (START, GRAD + UP, 1, 3),
        (START, GRAD + MID, 1, 1),
    ],
    (AT_ATTENDED_GRAD, 1): [
        (DONE, GRAD + MID, 1, 0),
        (DONE, GRAD + MID, 1, 1),
        (START, GRAD + MID, 1, 2),
        (START, GRAD + QKV, 1, 0),
    ],
    (AT_HIDDEN_GRAD, 0): [
        (DONE, GRAD + DOWN, 1, 3),
        (DONE, GRAD + UP, 1, 3),
        (START, GRAD + DOWN, 0, 0),
        (START, GRAD + QKV, 1, 1),
        (START, GRAD + DOWN, 1, 4),
        (START, GRAD + UP, 1, 4),
    ],
    (AT_MLP_GRAD, 0): [
        (DONE, GRAD + MID, 1, 2),
        (DONE, GRAD + QKV, 1, 0),
        (START, GRAD + QKV, 1, 2),
        (START, GRAD + DOWN, 0, 1),
        (START, GRAD + MID, 1, 3),
    ],
    (AT_CROSS_GRAD, 0): [
        (DONE, GRAD + DOWN, 0, 0),
        (DONE, GRAD + QKV, 1, 1),
        (START, GRAD + UP, 0, 0),
        (DONE, GRAD + DOWN, 1, 4),
        (DONE, GRAD + UP, 1, 4),
    ],
    (AT_CROSSED_GRAD, 0): [
        (DONE, GRAD + DOWN, 0, 1),
        (DONE, GRAD + QKV, 1, 2),
        (DONE, GRAD + MID, 1, 3),
        (START, GRAD + DOWN, 0, 2),
        (START, GRAD + UP, 0, 1),
        (START, GRAD + QKV, 1, 3),
        (START, GRAD + MID, 1, 4),
    ],
    (AT_SELF_GRAD, 0): [
        (DONE, GRAD + UP, 0, 0),
        (START, GRAD + UP, 0, 2),
        (START, GRAD + MID, 0, 0),
        (START, GRAD + TEXT, 0, 0),
    ],
    (AT_SELF_GRAD_NEXT, 0): [
        (DONE, GRAD + DOWN, 0, 2),
        (DONE, GRAD + UP, 0, 1),
        (DONE, GRAD + QKV, 1, 3),
        (DONE, GRAD + MID, 1, 4),
        (START, GRAD + DOWN, 0, 3),
        (START, GRAD + MID, 0, 1),
        (START, GRAD + TEXT, 0, 1),
        (START, GRAD + QKV, 1, 4),
    ],
    (AT_ATTENDED_GRAD, 0): [
        (DONE, GRAD + UP, 0, 2),
        (DONE, GRAD + MID, 0, 0),
        (DONE, GRAD + TEXT, 0, 0),
        (DONE, GRAD + DOWN, 0, 3),
        (START, GRAD + QKV, 0, 0),
        (START, GRAD + QKV, 0, 1),
        (START, GRAD + MID, 0, 2),
        (START, GRAD + TEXT, 0, 2),
        (START, GRAD + UP, 0, 3),
        (START, GRAD + DOWN, 0, 4),
    ],
}
first_modes = {
    (SMALL, 0): ALONG_DP,
    (QKV, 0): FULL,
    (MID, 0): FULL,
    (TEXT, 0): FULL,
    (UP, 0): NEAR,
    (DOWN, 0): NEAR,
    (QKV, 1): NEAR,
    (MID, 1): NEAR,
}


def frame_embedding(frames, feature, width, step):
    half = width // 2
    frequency = jnp.exp(-math.log(10000.0) * (feature % half).astype(jnp.float32) / half)
    is_sin = (feature < half)[None]
    span = min(32, frames)

    def turns(position):
        angles = position.astype(jnp.float32)[:, None] * frequency
        return (jnp.sin(angles), jnp.cos(angles))

    sin_high, cos_high = turns(jnp.arange(frames // span) * span)
    sin_low, cos_low = turns(jnp.arange(span))
    sin_step, cos_step = turns(step[None])
    times_cos = jnp.where(is_sin, sin_high, cos_high)[:, None]
    times_sin = jnp.where(is_sin, cos_high, -sin_high)[:, None]
    table = times_cos * cos_low[None] + times_sin * sin_low[None]
    return table.reshape(frames, width) + jnp.where(is_sin, sin_step, cos_step)


def gelu_parts(hidden):
    scale = math.sqrt(2.0 / math.pi)
    square = hidden * hidden
    bend = jnp.tanh(scale * (hidden + 0.044715 * (square * hidden)))
    half_up = 0.5 * (1.0 + bend)
    slope = half_up + 0.5 * hidden * (1.0 - bend * bend) * scale * (1.0 + 3.0 * 0.044715 * square)
    return (as_low(hidden * half_up), as_low(slope))


def dot_tn(left, right):
    return lax.dot_general(
        left, right, (((0,), (0,)), ((), ())), preferred_element_type=jnp.float32
    )


def adam_update(master, first_moment, second_moment, average, gradient, factor, step_rate):
    clipped = gradient * factor
    first_new = beta_first * first_moment + (1.0 - beta_first) * clipped
    second_new = beta_second * second_moment + (1.0 - beta_second) * clipped * clipped
    first_hat = first_new / (1.0 - beta_first**STEP)
    second_hat = second_new / (1.0 - beta_second**STEP)
    master_new = master - step_rate * (
        first_hat / (jnp.sqrt(second_hat) + adam_eps) + weight_decay * master
    )
    return (
        master_new,
        first_new,
        second_new,
        average_keep * average + (1.0 - average_keep) * master_new,
    )


def local(
    latents,
    noise_draw,
    timesteps,
    text_ids,
    text_len,
    item_counts,
    text_table,
    io_weight,
    io_first,
    io_second,
    io_average,
    norm_gains,
    gains_first,
    gains_second,
    gains_average,
    col_weight,
    col_first,
    col_second,
    col_average,
    text_weight,
    text_first,
    text_second,
    text_average,
    row_weight,
    row_first,
    row_second,
    row_average,
):
    items, channels, frame_part = latents.shape
    layout = Layout()
    group = layout.items * layout.ranks
    frames = frame_part * group
    levels, block = col_weight.shape[0], col_weight.shape[1]
    part = col_weight.shape[3]
    model_width = block * layout.dp_size
    gain_count = norm_gains.shape[0]
    text_block = text_weight.shape[1]
    item = layout.item

    table_rows = text_table.shape[0]
    local_ids = text_ids - (item * layout.ranks + layout.rank) * table_rows
    inside = (local_ids >= 0) & (local_ids < table_rows)
    picked = text_table[jnp.clip(local_ids, 0, table_rows - 1)]
    picked = jnp.where(inside[..., None], picked, jnp.zeros_like(picked))
    length = lax.dynamic_slice_in_dim(text_len, item, 1)

    steps = timesteps[item]
    alpha_bar = jnp.sum(jnp.where(steps == jnp.arange(1000), plan(), 0.0))
    alpha_all = jnp.sum(
        jnp.where(timesteps[:, None] == jnp.arange(1000)[None, :], plan()[None, :], 0.0), -1
    )
    noisy = (
        jnp.sqrt(alpha_all)[:, None, None] * latents
        + jnp.sqrt(1.0 - alpha_all)[:, None, None] * noise_draw
    )
    frames_all = lax.all_gather(
        jnp.concatenate([noisy, noise_draw], 1), MODEL, axis=2, tiled=True
    )
    frames_all = lax.dynamic_index_in_dim(frames_all, item, 0, keepdims=False)
    noisy, noise = as_low(frames_all[:channels]), frames_all[channels:]
    feature = (layout.blocks()[:, None] * block + jnp.arange(block)[None]).reshape(model_width)
    embedding = frame_embedding(frames, feature, model_width, steps)

    col_low, row_low, text_low = as_low(col_weight), as_low(row_weight), as_low(text_weight)
    small = jnp.concatenate(
        [
            as_low(io_weight).reshape(2 * channels, block),
            as_low(norm_gains),
            jnp.full((1, block), item_counts[0], jnp.bfloat16),
        ],
        0,
    )
    shards = {
        (SMALL, 0): small,
        (TEXT, 0): jnp.swapaxes(text_low, 0, 1).reshape(text_block, 2 * levels * part),
    }
    for level in range(levels):
        shards[QKV, level] = col_low[level, :, 0:3].reshape(block, 3 * part)
        shards[MID, level] = jnp.stack(
            [row_low[level, 0], col_low[level, :, 3], row_low[level, 1]]
        )
        shards[UP, level] = col_low[level, :, 4:].reshape(block, -1)
        shards[DOWN, level] = jnp.swapaxes(row_low[level, 2:], 0, 1).reshape(block, -1)
    names = [(SMALL, 0), (QKV, 0), (MID, 0), (TEXT, 0), (UP, 0), (DOWN, 0)]
    for level in range(1, levels):
        names += [(QKV, level), (MID, level), (UP, level), (DOWN, level)]
    kernel_names = [name for name in names if name in first_modes]
    chunks = [
        Chunk(shards[name].shape, first_modes[name], names.index(name) % 2 == 0)
        for name in kernel_names
    ]
    gathered = dict(
        zip(
            kernel_names,
            gather_first(
                layout,
                [shards[name] for name in kernel_names],
                chunks,
                [noisy, noise, embedding, picked],
            ),
        )
    )
    flow = Flow()
    weights = {}
    for name in names[1:]:
        axis = 1 if name[0] == MID else 0
        if first_modes.get(name) == FULL:
            pair = [gathered[name][index] for index in range(items)]
            if axis == 1:
                weights[name] = [
                    [half[:, index].reshape(model_width, part) for index in range(3)]
                    for half in pair
                ]
            else:
                weights[name] = [half.reshape((-1,) + half.shape[2:]) for half in pair]
            continue
        near, early = shards[name], layout.masks[:-1]
        if name in gathered:
            near, early = gathered[name], []
            near = near.reshape((-1,) + near.shape[2:]) if axis == 0 else near.swapaxes(0, 1)
        near = near.reshape((3, -1, part)) if axis == 1 else near
        flow.add(name, Gather(layout, near, axis, names.index(name) % 2 == 0, early))
    for name, chunk in flow.chunks.items():
        if name[1] == 0 or chunk.early:
            chunk.send(0, chunk.source(0))

    def weight(name, level):
        if (name, level) not in weights:
            weights[name, level] = flow.chunks[name, level].finish()
        return weights[name, level]

    small = jnp.swapaxes(gathered[SMALL, 0], 0, 1)
    small = small.reshape(2 * channels + gain_count + 1, model_width)
    io_w = [small[:channels], small[channels : 2 * channels]]
    gain_w = small[2 * channels : 2 * channels + gain_count].astype(jnp.float32)
    item_total = jnp.sum(small[-1].astype(jnp.float32)) / block
    text_w = weights[TEXT, 0]

    text_feat = lax.dynamic_index_in_dim(lax.psum(picked, MODEL), item, 0, keepdims=False)
    tokens = text_feat.shape[0]
    text_feat = jnp.take(
        text_feat.reshape(tokens, layout.dp_size, text_block), layout.blocks(), axis=1
    ).reshape(tokens, layout.dp_size * text_block)
    resid = dot_tn(noisy, io_w[0]) + embedding

    text_kv = [as_low(dot_nn(text_feat, weight)) for weight in text_w]

    kept_all = []
    part_sum = None
    for level in range(levels):
        resid_self, normed_self = norm_forward(resid, gain_w[3 * level], part_sum)
        qkv = [as_low(dot_nn(normed_self, w)) for w in weight(QKV, level)]
        qkv = flow.at((AT_ATTEND, level), qkv)
        attended, self_log = [None] * items, [None] * items
        for index in range(items):
            if index:
                qkv[index:] = flow.at((AT_ATTEND_NEXT, level), qkv[index:])
            whole = qkv[index]
            attended[index], self_log[index] = attend_forward(
                length, whole, 0, whole, part, whole, 2 * part, part, False
            )
        total = add_terms([dot_nt(o, w[0]) for o, w in zip(attended, weight(MID, level))])
        (part_sum,) = flow.at((AT_ATTENDED, level), [as_low(total)])
        resid_cross, normed_cross = norm_forward(resid_self, gain_w[3 * level + 1], part_sum)
        cross_query = [as_low(dot_nn(normed_cross, w[1])) for w in weight(MID, level)]
        cross_query = flow.at((AT_CROSS, level), cross_query)
        key_at = 2 * level * part
        cross_out, cross_log = [], []
        for query, text in zip(cross_query, text_kv):
            out, log = attend_forward(
                length, query, 0, text, key_at, text, key_at + part, part, True
            )
            cross_out.append(out)
            cross_log.append(log)
        total = add_terms([dot_nt(o, w[2]) for o, w in zip(cross_out, weight(MID, level))])
        (part_sum,) = flow.at((AT_CROSSED, level), [as_low(total)])
        resid_mlp, normed_mlp = norm_forward(resid_cross, gain_w[3 * level + 2], part_sum)
        active, slope = [], []
        for w in weight(UP, level):
            low_value, low_slope = gelu_parts(dot_nn(normed_mlp, w))
            active.append(low_value)
            slope.append(low_slope)
        active = flow.at((AT_ACTIVE, level), active)
        total = add_terms([dot_nt(a, w) for a, w in zip(active, weight(DOWN, level))])
        (part_sum,) = flow.at((AT_MLP, level), [as_low(total)])
        resid = resid_mlp
        kept_all.append(
            (
                (resid_self, normed_self, qkv, attended, self_log),
                (resid_cross, normed_cross, cross_query, cross_out, cross_log),
                (resid_mlp, normed_mlp, active, slope),
            )
        )
    resid, final_low = norm_forward(resid, gain_w[3 * levels], part_sum)
    predicted = dot_nt(io_w[1], final_low)
    residual_error = predicted - noise
    snr_ratio = alpha_bar / (1.0 - alpha_bar)
    loss_weight = jnp.minimum(snr_ratio, snr_limit) / snr_ratio
    valid = (item < item_counts[0]).astype(jnp.float32)
    item_scale = valid * loss_weight / (channels * frames)
    loss_part = item_scale * jnp.sum(residual_error * residual_error)
    pred_grad = as_low((2.0 * item_scale / item_total) * residual_error)
    out_proj_grad = dot_nn(pred_grad, final_low)
    final_grad = dot_tn(pred_grad, io_w[1])

    gain_grads = [None] * gain_count
    resid_grad, branch_grad, gain_grads[3 * levels] = norm_backward(
        resid, gain_w[3 * levels], final_grad
    )
    text_grads = [[None] * levels for _ in range(items)]
    for level in reversed(range(levels)):
        kept_self, kept_cross, kept_mlp = kept_all[level]
        resid_mlp, normed_mlp, active, slope = kept_mlp
        flow.add(
            (GRAD + DOWN, level),
            Scatter(layout, [as_low(dot_tn(branch_grad, a)) for a in active], False),
        )
        hidden_grad = [
            as_low(dot_nn(branch_grad, w) * s.astype(jnp.float32))
            for w, s in zip(weight(DOWN, level), slope)
        ]
        hidden_grad = flow.at((AT_HIDDEN_GRAD, level), hidden_grad)
        flow.add(
            (GRAD + UP, level),
            Scatter(layout, [as_low(dot_tn(normed_mlp, z)) for z in hidden_grad], True),
        )
        total = add_terms([dot_nt(z, w) for z, w in zip(hidden_grad, weight(UP, level))])
        (upstream,) = flow.at((AT_MLP_GRAD, level), [as_low(total)])
        resid_grad, branch_grad, gain_grads[3 * level + 2] = norm_backward(
            resid_mlp, gain_w[3 * level + 2], upstream, resid_grad
        )

        resid_cross, normed_cross, cross_query, cross_out, cross_log = kept_cross
        key_at = 2 * level * part
        out_grads = [as_low(dot_nn(branch_grad, w[2])) for w in weight(MID, level)]
        out_grads = flow.at((AT_CROSS_GRAD, level), out_grads)
        cross_w_grad, query_w_grad, query_grads = ([None] * items for _ in range(3))
        for index in reversed(range(items)):
            text = text_kv[index]
            query_grads[index], text_grads[index][level] = attend_backward(
                length,
                cross_query[index],
                0,
                text,
                key_at,
                text,
                key_at + part,
                cross_out[index],
                out_grads[index],
                cross_log[index],
                part,
                True,
            )
            cross_w_grad[index] = dot_tn(branch_grad, cross_out[index])
            query_w_grad[index] = dot_tn(normed_cross, query_grads[index])
        total = add_terms([dot_nt(q, w[1]) for q, w in zip(query_grads, weight(MID, level))])
        (upstream,) = flow.at((AT_CROSSED_GRAD, level), [as_low(total)])
        resid_grad, branch_grad, gain_grads[3 * level + 1] = norm_backward(
            resid_cross, gain_w[3 * level + 1], upstream, resid_grad
        )
        if level == 0:
            flow.add(
                (GRAD + TEXT, 0),
                Scatter(
                    layout,
                    [as_low(dot_tn(text_feat, jnp.concatenate(g, 1))) for g in text_grads],
                    True,
                ),
            )

        resid_self, normed_self, qkv, attended, self_log = kept_self
        self_w_grad = [dot_tn(branch_grad, o) for o in attended]
        flow.add(
            (GRAD + MID, level),
            Scatter(
                layout,
                [
                    as_low(jnp.concatenate(three, 1))
                    for three in zip(self_w_grad, query_w_grad, cross_w_grad)
                ],
                False,
            ),
        )
        out_grads = [as_low(dot_nn(branch_grad, w[0])) for w in weight(MID, level)]
        out_grads = flow.at((AT_SELF_GRAD, level), out_grads)
        qkv_grads = [None] * items
        for index in reversed(range(items)):
            if index == 0:
                out_grads[:1] = flow.at((AT_SELF_GRAD_NEXT, level), out_grads[:1])
            whole = qkv[index]
            (qkv_grads[index],) = attend_backward(
                length,
                whole,
                0,
                whole,
                part,
                whole,
                2 * part,
                attended[index],
                out_grads[index],
                self_log[index],
                part,
                False,
            )
        flow.add(
            (GRAD + QKV, level),
            Scatter(
                layout, [as_low(dot_tn(normed_self, z)) for z in qkv_grads], level > 0
            ),
        )
        total = add_terms([dot_nt(z, w) for z, w in zip(qkv_grads, weight(QKV, level))])
        (upstream,) = flow.at((AT_ATTENDED_GRAD, level), [as_low(total)])
        resid_grad, branch_grad, gain_grads[3 * level] = norm_backward(
            resid_self, gain_w[3 * level], upstream, resid_grad
        )

    down_g, up_g, mid_g, qkv_g = (
        [flow.chunks[name, level].finish() for level in range(levels)]
        for name in (GRAD + DOWN, GRAD + UP, GRAD + MID, GRAD + QKV)
    )
    text_g = flow.chunks[GRAD + TEXT, 0].finish()
    in_proj_grad = dot_nn(noisy, branch_grad)
    small_grad = jnp.concatenate([in_proj_grad, out_proj_grad, jnp.stack(gain_grads)], 0)
    small_grad = small_grad.reshape(-1, layout.dp_size, block).swapaxes(0, 1)
    small_grad = Scatter(layout, [small_grad, small_grad], False).finish()[0]

    io_grad = small_grad[: 2 * channels].reshape(2, channels, block)
    gain_grad = small_grad[2 * channels :]
    col_grad = jnp.stack(
        [
            jnp.concatenate(
                [
                    qkv_g[level].reshape(block, 3, part),
                    mid_g[level][:, None, part : 2 * part],
                    up_g[level].reshape(block, -1, part),
                ],
                1,
            )
            for level in range(levels)
        ]
    )
    kv_grad = jnp.swapaxes(text_g.reshape(text_block, levels, 2, part), 0, 1)
    row_grad = jnp.stack(
        [
            jnp.concatenate(
                [
                    mid_g[level][None, :, :part],
                    mid_g[level][None, :, 2 * part :],
                    jnp.swapaxes(down_g[level].reshape(block, -1, part), 0, 1),
                ],
                0,
            )
            for level in range(levels)
        ]
    )

    first_owner = (item * layout.ranks + layout.rank == 0).astype(jnp.float32)
    square = add_terms(
        [
            jnp.sum(grad * grad)
            for group in (qkv_g, mid_g, up_g, down_g, [text_g])
            for grad in group
        ]
    )
    square = square + first_owner * jnp.sum(small_grad * small_grad)
    loss_part = loss_part * (layout.rank == 0).astype(jnp.float32)
    totals = all_totals(layout, jnp.stack([square, loss_part]))
    grad_norm = jnp.sqrt(totals[0])
    factor = jnp.minimum(1.0, clip_limit / (grad_norm + 1e-06))
    results = [totals[1], item_total, grad_norm]
    io_updated = adam_update(
        io_weight, io_first, io_second, io_average, io_grad, factor, matrix_rate
    )
    results.extend(
        [io_updated[0], io_updated[1], io_updated[2][0], io_updated[2][1], io_updated[3]]
    )
    results.extend(
        adam_update(
            norm_gains, gains_first, gains_second, gains_average, gain_grad, factor, gain_rate
        )
    )
    results.extend(
        adam_update(col_weight, col_first, col_second, col_average, col_grad, factor, matrix_rate)
    )
    results.extend(
        adam_update(
            text_weight, text_first, text_second, text_average, kv_grad, factor, matrix_rate
        )
    )
    results.extend(
        adam_update(row_weight, row_first, row_second, row_average, row_grad, factor, row_rate)
    )
    return tuple(results)


def solution(mesh):
    def step(*arguments):
        dp_size = mesh.shape[DP]
        items = arguments[0].shape[0] // dp_size
        devices = mesh.devices.reshape(dp_size, items, -1)
        return jax.shard_map(
            local,
            mesh=Mesh(devices, (DP, ITEM, RANK)),
            in_specs=(
                P(DP, None, MODEL),
                P(DP, None, MODEL),
                P(DP),
                P(DP, None),
                P(DP),
                P(DP),
                P(MODEL, None),
                P(None, None, DP),
                P(None, None, DP),
                P(None, None, DP),
                P(None, None, DP),
                P(None, DP),
                P(None, DP),
                P(None, DP),
                P(None, DP),
                P(None, DP, None, MODEL),
                P(None, DP, None, MODEL),
                P(None, DP, None, MODEL),
                P(None, DP, None, MODEL),
                P(None, DP, None, MODEL),
                P(None, DP, None, MODEL),
                P(None, DP, None, MODEL),
                P(None, DP, None, MODEL),
                P(None, None, DP, MODEL),
                P(None, None, DP, MODEL),
                P(None, None, DP, MODEL),
                P(None, None, DP, MODEL),
            ),
            out_specs=(
                P(),
                P(),
                P(),
                P(None, None, DP),
                P(None, None, DP),
                P(None, DP),
                P(None, DP),
                P(None, None, DP),
                P(None, DP),
                P(None, DP),
                P(None, DP),
                P(None, DP),
                P(None, DP, None, MODEL),
                P(None, DP, None, MODEL),
                P(None, DP, None, MODEL),
                P(None, DP, None, MODEL),
                P(None, DP, None, MODEL),
                P(None, DP, None, MODEL),
                P(None, DP, None, MODEL),
                P(None, DP, None, MODEL),
                P(None, None, DP, MODEL),
                P(None, None, DP, MODEL),
                P(None, None, DP, MODEL),
                P(None, None, DP, MODEL),
            ),
            check_vma=False,
        )(*arguments)

    return step
```

time: 1200 us -> 1160 us (0.967)
  waiting for transfers between devices: 385 us -> 143 us
  Pallas kernels: 237 us -> 385 us
  local copies, waits for them, and re-layouts: 75.7 us -> 170 us
  blocking collectives: 48.8 us -> 7.55 us
  starting transfers between devices: 98.2 us -> 86 us
    ppermute x100 -> x72, waiting for transfers between devices: 385 us -> 142 us  [exchange(): return lax.ppermute(tensor, axis, [(i, i ^ mask) for i in range(size)])]
    pallas_call x30 -> x51, Pallas kernels: 237 us -> 385 us  [the longest x1 116 us: gather_first(): pl.pallas_call(after(len(waits), functools.partial(gather_kernel, layout....]
    unnamed x522 -> x587, local copies, waits for them, and re-layouts: 33 us -> 97.5 us
    psum x1 -> x0, blocking collectives: 37.3 us -> none  [local(): totals = lax.psum(jnp.stack([square, loss_part]), ('dp', 'mp'))]
    dot_general x28, matrix products: 93.4 us -> 61.7 us  [dot_tn(): lax.dot_general(left, right, (((0,), (0,)), ((), ())), preferred_element_...]
    dot_general x25, matrix products: 40.5 us -> 61.2 us  [dot_nt(): lax.dot_general(left, right, (((1,), (1,)), ((), ())), preferred_element_...]
    dot_general x28, matrix products: 60.8 us -> 76.9 us  [dot_nn(): return jnp.dot(left, right, preferred_element_type=jnp.float32)]
    slice x13 -> x26, local copies, waits for them, and re-layouts: 11.2 us -> 26.6 us  [the longest x9 12 us: __init__(): part[half:]]
  transfers between devices with their start and end apart: 101 -> 73, of which waited for: 45 -> 22; matrix products, arithmetic and copies ran while one was open for 26% -> 25% of each run, Pallas kernels for 17% -> 18%
where the time goes in v2:
time: 1160 us; the launch traced here: 1150 us
  Pallas kernels  385 us (33%)
  matrix products  200 us (17%)
  local copies, waits for them, and re-layouts  170 us (15%)
  waiting for transfers between devices  143 us (12%)
  other arithmetic  127 us (11%)
  starting transfers between devices  86 us (7%)
  between operations  32 us (3%)
    ppermute x72, waiting for transfers between devices, exchange(): return lax.ppermute(tensor, axis, [(i, i ^ mask) for i in range(size)])  142 us
    pallas_call x1, Pallas kernels, gather_first(): pl.pallas_call(after(len(waits), functools.partial(gather_kernel, layout....  116 us
    unnamed x587, local copies, waits for them, and re-layouts  97.5 us
    pallas_call x8, Pallas kernels, attend_backward(): pl.pallas_call(after(len(waits), functools.partial(attend_backward_kernel...  93.7 us
    ppermute x72, starting transfers between devices, exchange(): return lax.ppermute(tensor, axis, [(i, i ^ mask) for i in range(size)])  86 us
    pallas_call x8, Pallas kernels, attend_forward(): pl.pallas_call(after(len(waits), functools.partial(attend_forward_kernel,...  83.1 us
    dot_general x28, matrix products, dot_nn(): return jnp.dot(left, right, preferred_element_type=jnp.float32)  76.9 us
    dot_general x28, matrix products, dot_tn(): lax.dot_general(left, right, (((0,), (0,)), ((), ())), preferred_element_...  61.7 us
  transfers between devices with their start and end apart: 73, of which 22 were waited for; matrix products, arithmetic and copies ran while one was open for 25% of the time, Pallas kernels for 18%

profile of v2, /device:TPU:0, one launch (start us, length us, event | category | flops | bytes accessed | tf_op | source)
XLA Modules:
  0.0 1151.0 jit_solution(4368745591320073326)
XLA Ops:
  19.8 7.6 all_gather.3
  32.7 7.5 gather_fusion
  43.3 116.1 %gather_first.1 = (bf16[8,48,128]{2,1,0:T(8,128)(2,1)S(1)}, bf16[2,8,128,768]{3,2,1,0:T(8,128)(2,1)S(1)}, bf16[2,8,3,128,256]{4,3,2,1,0:T(8,128)(2,1)S(1)}, bf16...) custom-call(bf16[20,1024]{1,0:T(8,128)(2,1)S(1)} %copy-done.79, ...), custom_call_target="tpu_custom_call" | custom-call | flops 10000 | bytes 100000000 | tf_op jit(solution)/shard_map/gather_first/pallas_call | solution.py:363
  196.4 14.2 %attend_fwd.8 = (bf16[1024,256]{1,0:T(8,128)(2,1)S(1)}, f32[2,8,1024]{2,1,0:T(8,128)S(1)}) custom-call(s32[1]{0:T(128)} %dynamic_slice.16.refs_0_, bf16[1024,768]{1,0:T(8,128)(2,1)S(1)} %convolution_convert_fusion.17.refs_1_.refs_2_.refs_3_, bf16[1024,768]{1,0:T(8,128)(2,1)S(1)} %convolution_convert_fusion.17.refs_1_.refs_2_.refs_3_, ...), custom_call_target="tpu_custom_call" | custom-call | flops 4294967296 | bytes 2097152 | tf_op jit(solution)/shard_map/attend_fwd/pallas_call | solution.py:695
  212.1 14.3 %attend_fwd.9 = (bf16[1024,256]{1,0:T(8,128)(2,1)S(1)}, f32[2,8,1024]{2,1,0:T(8,128)S(1)}) custom-call(s32[1]{0:T(128)} %dynamic_slice.16.refs_0_, bf16[1024,768]{1,0:T(8,128)(2,1)S(1)} %convolution_convert_fusion.16.refs_1_.refs_2_.refs_3_, bf16[1024,768]{1,0:T(8,128)(2,1)S(1)} %convolution_convert_fusion.16.refs_1_.refs_2_.refs_3_, ...), custom_call_target="tpu_custom_call" | custom-call | flops 4294967296 | bytes 2097152 | tf_op jit(solution)/shard_map/attend_fwd/pallas_call | solution.py:695
  249.1 12.7 %collective-permute-start.8 = (bf16[256,1024]{1,0:T(8,128)(2,1)}, bf16[256,1024]{1,0:T(8,128)(2,1)S(1)}, u32[]{:S(2)}, u32[]{:S(2)}) collective-permute-start(bf16[256,1024]{1,0:T(8,128)(2,1)} %get-tuple-element.193), channel_id=1, source_target_pairs={{0,8},{4,12},{8,0},{12,4},{16,24},{20,28},{24,16},{28,20},{1,9},{5... | collective-permute-start | bytes 1572872 | tf_op jit(solution)/shard_map/ppermute | solution.py:69
  365.7 14.3 %attend_fwd.12 = (bf16[1024,256]{1,0:T(8,128)(2,1)S(1)}, f32[2,8,1024]{2,1,0:T(8,128)S(1)}) custom-call(s32[1]{0:T(128)} %dynamic_slice.16.refs_0_, bf16[1024,768]{1,0:T(8,128)(2,1)S(1)} %copy-done.45, bf16[1024,768]{1,0:T(8,128)(2,1)S(1)} %copy-done.45, bf16[1024,768]{1,0:T(8,128)(2,1)S(1)} %copy-done.45), custom_call_target="tpu_custom_call" | custom-call | flops 4294967296 | bytes 2097152 | tf_op jit(solution)/shard_map/attend_fwd/pallas_call | solution.py:695
  380.0 14.3 %attend_fwd.13 = (bf16[1024,256]{1,0:T(8,128)(2,1)S(1)}, f32[2,8,1024]{2,1,0:T(8,128)S(1)}) custom-call(s32[1]{0:T(128)} %dynamic_slice.16.refs_0_, bf16[1024,768]{1,0:T(8,128)(2,1)S(1)} %copy-done.47, bf16[1024,768]{1,0:T(8,128)(2,1)S(1)} %copy-done.47, bf16[1024,768]{1,0:T(8,128)(2,1)S(1)} %copy-done.47), custom_call_target="tpu_custom_call" | custom-call | flops 4294967296 | bytes 2097152 | tf_op jit(solution)/shard_map/attend_fwd/pallas_call | solution.py:695
  474.9 9.5 multiply_convert_fusion.2.refs_1_
  514.3 7.5 norm_swap_bwd.6
  542.2 13.5 %collective-permute-done.22.refs_4_ = bf16[512,1024]{1,0:T(8,128)(2,1)} collective-permute-done((bf16[512,1024]{1,0:T(8,128)(2,1)}, bf16[512,1024]{1,0:T(8,128)(2,1)}, u32[]{:S(2)}, u32[]{:S(2)}) %collective-permute-start.22) | collective-permute-done | bytes 1048608 | tf_op jit(solution)/shard_map/ppermute | solution.py:69
  591.7 7.5 norm_swap_bwd.7
  615.4 13.8 %collective-permute-done.25.refs_3_ = bf16[512,1024]{1,0:T(8,128)(2,1)} collective-permute-done((bf16[512,1024]{1,0:T(8,128)(2,1)}, bf16[512,1024]{1,0:T(8,128)(2,1)}, u32[]{:S(2)}, u32[]{:S(2)}) %collective-permute-start.25) | collective-permute-done | bytes 1048608 | tf_op jit(solution)/shard_map/ppermute | solution.py:69
  629.9 20.9 %collective-permute-done.26.refs_4_ = bf16[512,1024]{1,0:T(8,128)(2,1)} collective-permute-done((bf16[512,1024]{1,0:T(8,128)(2,1)}, bf16[512,1024]{1,0:T(8,128)(2,1)}, u32[]{:S(2)}, u32[]{:S(2)}) %collective-permute-start.26) | collective-permute-done | bytes 1048608 | tf_op jit(solution)/shard_map/ppermute | solution.py:69
  659.1 16.2 %attend_bwd.11 = bf16[1024,768]{1,0:T(8,128)(2,1)S(1)} custom-call(s32[1]{0:T(128)} %dynamic_slice.16.refs_0_, bf16[1024,768]{1,0:T(8,128)(2,1)S(1)} %copy-done.47, bf16[1024,768]{1,0:T(8,128)(2,1)S(1)} %copy-done.47, bf16[1024,768]{1,0:T(8,128)(2,1)S(1)} %copy-done.47, bf16[1024,256]{1,0:T(8,128)(2,1)S(1)} %get-tuple-element.208.refs_4_, ...), custom_call_target="tpu_custom_call" | custom-call | flops 10737418240 | bytes 4194304 | tf_op jit(solution)/shard_map/attend_bwd/pallas_call | solution.py:799
  677.3 16.7 %attend_bwd.10 = bf16[1024,768]{1,0:T(8,128)(2,1)S(1)} custom-call(s32[1]{0:T(128)} %dynamic_slice.16.refs_0_, bf16[1024,768]{1,0:T(8,128)(2,1)S(1)} %copy-done.46, bf16[1024,768]{1,0:T(8,128)(2,1)S(1)} %copy-done.46, bf16[1024,768]{1,0:T(8,128)(2,1)S(1)} %copy-done.46, bf16[1024,256]{1,0:T(8,128)(2,1)S(1)} %get-tuple-element.206.refs_4_, ...), custom_call_target="tpu_custom_call" | custom-call | flops 10737418240 | bytes 4194304 | tf_op jit(solution)/shard_map/attend_bwd/pallas_call | solution.py:799
  714.4 7.4 norm_swap_bwd.8
  779.1 16.0 %collective-permute-done.33.refs_4_ = bf16[512,768]{1,0:T(8,128)(2,1)S(1)} collective-permute-done((bf16[512,768]{1,0:T(8,128)(2,1)}, bf16[512,768]{1,0:T(8,128)(2,1)S(1)}, u32[]{:S(2)}, u32[]{:S(2)}) %collective-permute-start.33) | collective-permute-done | bytes 786464 | tf_op jit(solution)/shard_map/ppermute | solution.py:69
  894.6 16.4 %attend_bwd.15 = bf16[1024,768]{1,0:T(8,128)(2,1)S(1)} custom-call(s32[1]{0:T(128)} %dynamic_slice.16.refs_0_, bf16[1024,768]{1,0:T(8,128)(2,1)S(1)} %copy-done.133, bf16[1024,768]{1,0:T(8,128)(2,1)S(1)} %copy-done.133, bf16[1024,768]{1,0:T(8,128)(2,1)S(1)} %copy-done.133, bf16[1024,256]{1,0:T(8,128)(2,1)S(1)} %copy-done.59, ...), custom_call_target="tpu_custom_call" | custom-call | flops 10737418240 | bytes 4194304 | tf_op jit(solution)/shard_map/attend_bwd/pallas_call | solution.py:799
  928.0 16.3 %attend_bwd.14 = bf16[1024,768]{1,0:T(8,128)(2,1)S(1)} custom-call(s32[1]{0:T(128)} %dynamic_slice.16.refs_0_, bf16[1024,768]{1,0:T(8,128)(2,1)S(1)} %copy-done.131, bf16[1024,768]{1,0:T(8,128)(2,1)S(1)} %copy-done.131, bf16[1024,768]{1,0:T(8,128)(2,1)S(1)} %copy-done.131, bf16[1024,256]{1,0:T(8,128)(2,1)S(1)} %copy-done.63, ...), custom_call_target="tpu_custom_call" | custom-call | flops 10737418240 | bytes 4194304 | tf_op jit(solution)/shard_map/attend_bwd/pallas_call | solution.py:799
  961.7 8.6 norm_swap_bwd.11
  997.4 8.1 collective-permute-done.67
  1036.6 13.4 %collective-permute-done.63 = bf16[384,1024]{1,0:T(8,128)(2,1)} collective-permute-done((bf16[384,1024]{1,0:T(8,128)(2,1)}, bf16[384,1024]{1,0:T(8,128)(2,1)}, u32[]{:S(2)}, u32[]{:S(2)}) %collective-permute-start.63) | collective-permute-done | bytes 786464 | tf_op jit(solution)/shard_map/ppermute | solution.py:69
  1105.9 10.6 totals.1
  (1029 shorter events, 715.6 us)
Async XLA Ops:
  169.1 67.5 %all-reduce.4.cloned.1.call-start = ((), (), s32[]{:S(2)}) async-start(), calls=%async_computation | async-start | bytes 786432 | tf_op jit(solution)/shard_map/psum | solution.py:1153
  169.8 79.2 %collective-permute-start.4 = (bf16[512,1024]{1,0:T(8,128)(2,1)}, bf16[512,1024]{1,0:T(8,128)(2,1)}, u32[]{:S(2)}, u32[]{:S(2)}) collective-permute-start(bf16[512,1024]{1,0:T(8,128)(2,1)} %bitcast.356), channel_id=1, source_target_pairs={{0,4},{4,0},{8,12},{12,8},{16,20},{20,16},{24,28},{28,24},{1,5},{5... | collective-permute-start | bytes 3145736 | tf_op jit(solution)/shard_map/ppermute | solution.py:69
  171.1 77.9 %collective-permute-start = (bf16[512,1024]{1,0:T(8,128)(2,1)}, bf16[512,1024]{1,0:T(8,128)(2,1)}, u32[]{:S(2)}, u32[]{:S(2)}) collective-permute-start(bf16[512,1024]{1,0:T(8,128)(2,1)} %bitcast.357), channel_id=1, source_target_pairs={{0,2},{2,0},{1,3},{3,1},{4,6},{6,4},{5,7},{7,5},{8,10},{10,8},{9,1... | collective-permute-start | bytes 3145736 | tf_op jit(solution)/shard_map/ppermute | solution.py:69
  172.1 76.9 %collective-permute-start.5 = (bf16[512,1024]{1,0:T(8,128)(2,1)}, bf16[512,1024]{1,0:T(8,128)(2,1)}, u32[]{:S(2)}, u32[]{:S(2)}) collective-permute-start(bf16[512,1024]{1,0:T(8,128)(2,1)} %bitcast.360), channel_id=1, source_target_pairs={{0,2},{2,0},{1,3},{3,1},{4,6},{6,4},{5,7},{7,5},{8,10},{10,8},{9,1... | collective-permute-start | bytes 3145736 | tf_op jit(solution)/shard_map/ppermute | solution.py:69
  173.2 75.9 %collective-permute-start.1 = (bf16[512,1024]{1,0:T(8,128)(2,1)}, bf16[512,1024]{1,0:T(8,128)(2,1)}, u32[]{:S(2)}, u32[]{:S(2)}) collective-permute-start(bf16[512,1024]{1,0:T(8,128)(2,1)} %bitcast.361), channel_id=1, source_target_pairs={{0,4},{4,0},{8,12},{12,8},{16,20},{20,16},{24,28},{28,24},{1,5},{5... | collective-permute-start | bytes 3145736 | tf_op jit(solution)/shard_map/ppermute | solution.py:69
  175.6 65.2 %collective-permute-start.3 = (bf16[128,1024]{1,0:T(8,128)(2,1)}, bf16[128,1024]{1,0:T(8,128)(2,1)}, u32[]{:S(2)}, u32[]{:S(2)}) collective-permute-start(bf16[128,1024]{1,0:T(8,128)(2,1)} %bitcast.105), channel_id=1, source_target_pairs={{0,16},{4,20},{8,24},{12,28},{16,0},{20,4},{24,8},{28,12},{1,17},{... | collective-permute-start | bytes 786440 | tf_op jit(solution)/shard_map/ppermute | solution.py:69
  249.1 48.5 %collective-permute-start.8 = (bf16[256,1024]{1,0:T(8,128)(2,1)}, bf16[256,1024]{1,0:T(8,128)(2,1)S(1)}, u32[]{:S(2)}, u32[]{:S(2)}) collective-permute-start(bf16[256,1024]{1,0:T(8,128)(2,1)} %get-tuple-element.193), channel_id=1, source_target_pairs={{0,8},{4,12},{8,0},{12,4},{16,24},{20,28},{24,16},{28,20},{1,9},{5... | collective-permute-start | bytes 1572872 | tf_op jit(solution)/shard_map/ppermute | solution.py:69
  360.2 51.3 %collective-permute-start.18 = (bf16[512,1024]{1,0:T(8,128)(2,1)}, bf16[512,1024]{1,0:T(8,128)(2,1)}, u32[]{:S(2)}, u32[]{:S(2)}) collective-permute-start(bf16[512,1024]{1,0:T(8,128)(2,1)} %get-tuple-element.211), channel_id=1, source_target_pairs={{0,4},{4,0},{8,12},{12,8},{16,20},{20,16},{24,28},{28,24},{1,5},{5... | collective-permute-start | bytes 3145736 | tf_op jit(solution)/shard_map/ppermute | solution.py:69
  361.7 49.8 %collective-permute-start.16 = (bf16[512,1024]{1,0:T(8,128)(2,1)}, bf16[512,1024]{1,0:T(8,128)(2,1)}, u32[]{:S(2)}, u32[]{:S(2)}) collective-permute-start(bf16[512,1024]{1,0:T(8,128)(2,1)} %get-tuple-element.211), channel_id=1, source_target_pairs={{0,2},{2,0},{1,3},{3,1},{4,6},{6,4},{5,7},{7,5},{8,10},{10,8},{9,1... | collective-permute-start | bytes 3145736 | tf_op jit(solution)/shard_map/ppermute | solution.py:69
  362.5 49.1 %collective-permute-start.19 = (bf16[512,1024]{1,0:T(8,128)(2,1)}, bf16[512,1024]{1,0:T(8,128)(2,1)}, u32[]{:S(2)}, u32[]{:S(2)}) collective-permute-start(bf16[512,1024]{1,0:T(8,128)(2,1)} %get-tuple-element.212), channel_id=1, source_target_pairs={{0,2},{2,0},{1,3},{3,1},{4,6},{6,4},{5,7},{7,5},{8,10},{10,8},{9,1... | collective-permute-start | bytes 3145736 | tf_op jit(solution)/shard_map/ppermute | solution.py:69
  363.8 47.8 %collective-permute-start.17 = (bf16[512,1024]{1,0:T(8,128)(2,1)}, bf16[512,1024]{1,0:T(8,128)(2,1)}, u32[]{:S(2)}, u32[]{:S(2)}) collective-permute-start(bf16[512,1024]{1,0:T(8,128)(2,1)} %get-tuple-element.212), channel_id=1, source_target_pairs={{0,4},{4,0},{8,12},{12,8},{16,20},{20,16},{24,28},{28,24},{1,5},{5... | collective-permute-start | bytes 3145736 | tf_op jit(solution)/shard_map/ppermute | solution.py:69
  532.9 47.5 %collective-permute-start.23 = (bf16[512,1024]{1,0:T(8,128)(2,1)}, bf16[512,1024]{1,0:T(8,128)(2,1)}, u32[]{:S(2)}, u32[]{:S(2)}) collective-permute-start(bf16[512,1024]{1,0:T(8,128)(2,1)} %get-tuple-element.237), channel_id=1, source_target_pairs={{0,4},{4,0},{8,12},{12,8},{16,20},{20,16},{24,28},{28,24},{1,5},{5... | collective-permute-start | bytes 3145736 | tf_op jit(solution)/shard_map/ppermute | solution.py:69
  534.4 53.5 %collective-permute-start.24 = (bf16[512,1024]{1,0:T(8,128)(2,1)}, bf16[512,1024]{1,0:T(8,128)(2,1)}, u32[]{:S(2)}, u32[]{:S(2)}) collective-permute-start(bf16[512,1024]{1,0:T(8,128)(2,1)} %get-tuple-element.238), channel_id=1, source_target_pairs={{0,2},{2,0},{1,3},{3,1},{4,6},{6,4},{5,7},{7,5},{8,10},{10,8},{9,1... | collective-permute-start | bytes 3145736 | tf_op jit(solution)/shard_map/ppermute | solution.py:69
  604.9 48.3 %collective-permute-start.27 = (bf16[512,1024]{1,0:T(8,128)(2,1)}, bf16[512,1024]{1,0:T(8,128)(2,1)}, u32[]{:S(2)}, u32[]{:S(2)}) collective-permute-start(bf16[512,1024]{1,0:T(8,128)(2,1)} %get-tuple-element.245), channel_id=1, source_target_pairs={{0,2},{2,0},{1,3},{3,1},{4,6},{6,4},{5,7},{7,5},{8,10},{10,8},{9,1... | collective-permute-start | bytes 3145736 | tf_op jit(solution)/shard_map/ppermute | solution.py:69
  629.2 78.5 %collective-permute-start.28 = (bf16[512,768]{1,0:T(8,128)(2,1)}, bf16[512,768]{1,0:T(8,128)(2,1)}, u32[]{:S(2)}, u32[]{:S(2)}) collective-permute-start(bf16[512,768]{1,0:T(8,128)(2,1)} %get-tuple-element.250), channel_id=1, source_target_pairs={{0,2},{2,0},{1,3},{3,1},{4,6},{6,4},{5,7},{7,5},{8,10},{10,8},{9,1... | collective-permute-start | bytes 2359304 | tf_op jit(solution)/shard_map/ppermute | solution.py:69
  655.6 47.4 %collective-permute-start.30 = (bf16[256,1024]{1,0:T(8,128)(2,1)}, bf16[256,1024]{1,0:T(8,128)(2,1)S(1)}, u32[]{:S(2)}, u32[]{:S(2)}) collective-permute-start(bf16[256,1024]{1,0:T(8,128)(2,1)} %get-tuple-element.255), channel_id=1, source_target_pairs={{0,8},{4,12},{8,0},{12,4},{16,24},{20,28},{24,16},{28,20},{1,9},{5... | collective-permute-start | bytes 1572872 | tf_op jit(solution)/shard_map/ppermute | solution.py:69
  657.5 47.9 %collective-permute-start.31 = (bf16[256,1024]{1,0:T(8,128)(2,1)}, bf16[256,1024]{1,0:T(8,128)(2,1)S(1)}, u32[]{:S(2)}, u32[]{:S(2)}) collective-permute-start(bf16[256,1024]{1,0:T(8,128)(2,1)} %get-tuple-element.256), channel_id=1, source_target_pairs={{0,8},{4,12},{8,0},{12,4},{16,24},{20,28},{24,16},{28,20},{1,9},{5... | collective-permute-start | bytes 1572872 | tf_op jit(solution)/shard_map/ppermute | solution.py:69
  657.6 52.3 %collective-permute-start.29 = (bf16[512,768]{1,0:T(8,128)(2,1)}, bf16[512,768]{1,0:T(8,128)(2,1)}, u32[]{:S(2)}, u32[]{:S(2)}) collective-permute-start(bf16[512,768]{1,0:T(8,128)(2,1)} %get-tuple-element.251), channel_id=1, source_target_pairs={{0,2},{2,0},{1,3},{3,1},{4,6},{6,4},{5,7},{7,5},{8,10},{10,8},{9,1... | collective-permute-start | bytes 2359304 | tf_op jit(solution)/shard_map/ppermute | solution.py:69
  746.4 74.8 %collective-permute-start.35 = (bf16[512,768]{1,0:T(8,128)(2,1)}, bf16[512,768]{1,0:T(8,128)(2,1)}, u32[]{:S(2)}, u32[]{:S(2)}) collective-permute-start(bf16[512,768]{1,0:T(8,128)(2,1)} %get-tuple-element.265), channel_id=1, source_target_pairs={{0,4},{4,0},{8,12},{12,8},{16,20},{20,16},{24,28},{28,24},{1,5},{5... | collective-permute-start | bytes 2359304 | tf_op jit(solution)/shard_map/ppermute | solution.py:69
  770.0 51.2 %collective-permute-start.34 = (bf16[512,1024]{1,0:T(8,128)(2,1)}, bf16[512,1024]{1,0:T(8,128)(2,1)}, u32[]{:S(2)}, u32[]{:S(2)}) collective-permute-start(bf16[512,1024]{1,0:T(8,128)(2,1)} %get-tuple-element.264), channel_id=1, source_target_pairs={{0,2},{2,0},{1,3},{3,1},{4,6},{6,4},{5,7},{7,5},{8,10},{10,8},{9,1... | collective-permute-start | bytes 3145736 | tf_op jit(solution)/shard_map/ppermute | solution.py:69
  841.2 47.7 %collective-permute-start.41 = (bf16[512,1024]{1,0:T(8,128)(2,1)}, bf16[512,1024]{1,0:T(8,128)(2,1)}, u32[]{:S(2)}, u32[]{:S(2)}) collective-permute-start(bf16[512,1024]{1,0:T(8,128)(2,1)} %get-tuple-element.280), channel_id=1, source_target_pairs={{0,4},{4,0},{8,12},{12,8},{16,20},{20,16},{24,28},{28,24},{1,5},{5... | collective-permute-start | bytes 3145736 | tf_op jit(solution)/shard_map/ppermute | solution.py:69
  877.4 47.5 %collective-permute-start.44 = (bf16[512,1024]{1,0:T(8,128)(2,1)}, bf16[512,1024]{1,0:T(8,128)(2,1)}, u32[]{:S(2)}, u32[]{:S(2)}) collective-permute-start(bf16[512,1024]{1,0:T(8,128)(2,1)} %get-tuple-element.288), channel_id=1, source_target_pairs={{0,4},{4,0},{8,12},{12,8},{16,20},{20,16},{24,28},{28,24},{1,5},{5... | collective-permute-start | bytes 3145736 | tf_op jit(solution)/shard_map/ppermute | solution.py:69
  891.5 58.9 %collective-permute-start.46 = (bf16[512,768]{1,0:T(8,128)(2,1)}, bf16[512,768]{1,0:T(8,128)(2,1)}, u32[]{:S(2)}, u32[]{:S(2)}) collective-permute-start(bf16[512,768]{1,0:T(8,128)(2,1)} %get-tuple-element.294), channel_id=1, source_target_pairs={{0,2},{2,0},{1,3},{3,1},{4,6},{6,4},{5,7},{7,5},{8,10},{10,8},{9,1... | collective-permute-start | bytes 2359304 | tf_op jit(solution)/shard_map/ppermute | solution.py:69
  892.6 51.7 %collective-permute-start.47 = (bf16[384,1024]{1,0:T(8,128)(2,1)}, bf16[384,1024]{1,0:T(8,128)(2,1)}, u32[]{:S(2)}, u32[]{:S(2)}) collective-permute-start(bf16[384,1024]{1,0:T(8,128)(2,1)} %get-tuple-element.295), channel_id=1, source_target_pairs={{0,4},{4,0},{8,12},{12,8},{16,20},{20,16},{24,28},{28,24},{1,5},{5... | collective-permute-start | bytes 2359304 | tf_op jit(solution)/shard_map/ppermute | solution.py:69
  (332 other events, 3253.7 us)
Sparse Core Ops, SparseCore 0:
  172.9 43.3 all-reduce.3
